TPU v7x, 512 devices: a whole 4x8x8 slice. The times are simulated.
512 devices in a mesh: replica: 32 (over x_hi, z, core), fsdp: 16 (over x_lo, y).
Axes of the slice: x: 4 (x_hi: 2, x_lo: 2; x = x_hi * 2 + x_lo), y: 8, z: 8, core: 2. Of those that a mesh axis runs over, the one named last changes fastest.
Arguments:
- layer_input: bfloat16 [122880, 3072], P(('replica', 'fsdp')), may hold values from -24 to 24
- cotangent: bfloat16 [122880, 512], P(('replica', 'fsdp')), may hold values from -6 to 6
- local_weight: bfloat16 [32, 3072, 512], P('replica', 'fsdp'), may hold values from -0.21875 to 0.21875
- first_moment: float32 [32, 3072, 512], P('replica', 'fsdp'), may hold values from -128 to 128
- second_moment: float32 [32, 3072, 512], P('replica', 'fsdp'), may hold values from 100 to 10000
- anchor: float32 [3072, 512], P('fsdp', 'replica'), may hold values from -0.109375 to 0.109375
- outer_momentum: float32 [3072, 512], P('fsdp', 'replica'), may hold values from -0.3125 to 0.3125
Outputs:
- input_grad: bfloat16 [122880, 3072], P(('replica', 'fsdp'))
- new_weight: bfloat16 [32, 3072, 512], P('replica', 'fsdp')
- new_first: float32 [32, 3072, 512], P('replica', 'fsdp')
- new_second: float32 [32, 3072, 512], P('replica', 'fsdp')
- new_anchor: float32 [3072, 512], P('fsdp', 'replica')
- new_momentum: float32 [3072, 512], P('fsdp', 'replica')
All inputs are finite; a program needn't handle non-finite values.
Results may differ from a plain program's by a relative error of at most 0.012.
Values may be sent and summed in bfloat16 or wider, within the bound.
A program may use at most 64 MiB of HBM per device.

v0:
```python
import jax
import jax.numpy as jnp
from jax import lax
from jax.sharding import PartitionSpec as P

beta_one = 0.9
beta_two = 0.95
adam_eps = 1e-08
learn_rate = 0.0003
decay_rate = 0.1
outer_rate = 0.7
outer_mu = 0.9
blend_keep = 0.5


def body(layer_input, cotangent, local_weight, first_moment, second_moment, anchor, outer_momentum):
    weight_rows = local_weight[0]
    weights = weight_rows.astype(jnp.float32)
    total = lax.psum(weights.astype(jnp.bfloat16), "replica").astype(jnp.float32)
    share_width = anchor.shape[1]
    position = lax.axis_index("replica")
    share = lax.dynamic_slice_in_dim(total, position * share_width, share_width, 1)
    delta = anchor - share / lax.axis_size("replica")
    new_momentum = outer_mu * outer_momentum + delta
    new_anchor = anchor - outer_rate * (delta + outer_mu * new_momentum)
    gradient = lax.psum_scatter(
        lax.dot_general(
            layer_input, cotangent, (((0,), (0,)), ((), ())), preferred_element_type=jnp.float32
        ).astype(jnp.bfloat16),
        "fsdp",
        scatter_dimension=0,
        tiled=True,
    ).astype(jnp.float32)
    product = lax.dot_general(
        cotangent,
        lax.all_gather(weight_rows, "fsdp", axis=0, tiled=True),
        (((1,), (1,)), ((), ())),
        preferred_element_type=jnp.float32,
    )
    input_grad = product.astype(jnp.bfloat16)
    new_first = beta_one * first_moment[0] + (1.0 - beta_one) * gradient
    new_second = beta_two * second_moment[0] + (1.0 - beta_two) * gradient * gradient
    update = new_first / (jnp.sqrt(new_second) + adam_eps)
    inner = weights - learn_rate * (update + decay_rate * weights)
    full_anchor = lax.all_gather(new_anchor, "replica", axis=1, tiled=True)
    new_weight = (blend_keep * inner + (1.0 - blend_keep) * full_anchor).astype(jnp.bfloat16)
    return (
        input_grad,
        new_weight[None],
        new_first[None],
        new_second[None],
        new_anchor,
        new_momentum,
    )


def solution(mesh):
    in_specs = (
        P(("replica", "fsdp"), None),
        P(("replica", "fsdp"), None),
        P("replica", "fsdp", None),
        P("replica", "fsdp", None),
        P("replica", "fsdp", None),
        P("fsdp", "replica"),
        P("fsdp", "replica"),
    )
    out_specs = (
        P(("replica", "fsdp"), None),
        P("replica", "fsdp", None),
        P("replica", "fsdp", None),
        P("replica", "fsdp", None),
        P("fsdp", "replica"),
        P("fsdp", "replica"),
    )
    return jax.shard_map(body, mesh=mesh, in_specs=in_specs, out_specs=out_specs, check_vma=False)
```

profile of v0, /device:TPU:1, one launch (start us, length us, event | category | flops | bytes accessed | tf_op | source)
XLA Modules:
  0.0 351.7 jit_solution(6154416301743386509)
XLA Ops:
  8.0 0.0 copy-start
  8.0 0.0 all-reduce.2.cloned.1.call-start
  8.1 1.9 copy.34
  9.9 0.0 all-reduce.2.cloned.1.call-update
  10.0 0.0 all-gather.3.cloned.1.call-start
  10.0 0.5 all-gather.3.cloned.1.call-update
  10.5 0.0 reduce-scatter.4.cloned.1.call-start
  10.6 0.0 copy-done
  10.6 3.6 %convolution_convert_fusion = bf16[3072,512]{1,0:T(8,128)(2,1)} fusion(bf16[240,3072]{1,0:T(8,128)(2,1)S(1)} %copy-done, bf16[240,512]{1,0:T(8,128)(2,1)} %param.8), kind=kOutput, calls=%fused_computation | convolution fusion | flops 756547584 | bytes 4866048 | tf_op jit(solution)/shard_map/dot_general | solution.py:27
  14.2 0.0 copy-start.3
  14.2 0.0 copy-start.4
  14.2 0.0 copy-start.6
  14.2 0.0 copy-start.7
  14.2 0.0 copy-start.2
  14.3 0.0 reduce-scatter.4.cloned.1.call-update
  14.3 0.9 copy-done.3
  15.2 0.2 copy.37
  15.4 0.0 copy-done.4
  15.4 0.2 copy.35
  15.7 0.0 copy-start.1
  15.7 272.5 %all-reduce.2.cloned.1.call-done = bf16[192,512]{0,1:T(8,128)(2,1)} async-done(((bf16[192,512]{0,1:T(8,128)(2,1)}), bf16[192,512]{0,1:T(8,128)(2,1)}) %all-reduce.2.cloned.1.call-update) | async-done | bytes 196624 | tf_op jit(solution)/shard_map/psum | solution.py:19
  288.2 0.0 copy-done.6
  288.2 0.0 copy-done.7
  288.2 1.3 multiply_subtract_fusion
  289.5 0.0 copy-start.5
  289.5 0.6 copy-done.5
  290.1 41.3 %all_gather.7 = f32[192,512]{0,1:T(8,128)} all-gather(f32[192,16]{0,1:T(8,128)S(1)} %get-tuple-element.30), channel_id=1, replica_groups=mesh['replica'=32,'fsdp'=16] {'replica'}, dimensions={1}, use_global_device_ids=true | all-gather | bytes 405504 | tf_op jit(solution)/shard_map/all_gather | solution.py:45
  331.4 0.0 all-gather.3.cloned.1.call-done
  331.4 0.0 copy-done.2
  331.4 4.0 %convolution_convert_fusion.1 = bf16[240,3072]{1,0:T(8,128)(2,1)} fusion(bf16[240,512]{1,0:T(8,128)(2,1)S(1)} %copy-done.2, bf16[1,3072,512]{2,1,0:T(8,128)(2,1)} %all-gather.3.cloned.1.call-done), kind=kOutput, calls=%fused_computation.1 | convolution fusion | flops 755712000 | bytes 4866048 | tf_op jit(solution)/shard_map/dot_general | solution.py:34
  335.4 0.0 reduce-scatter.4.cloned.1.call-done
  335.4 1.8 copy.42
  337.1 0.0 copy-done.1
  337.2 2.4 fusion.9
  339.6 1.8 copy.38
  341.3 2.0 copy.39
  343.3 0.9 copy.40
Async XLA Ops:
  8.0 2.6 copy-start
  8.0 280.2 %all-reduce.2.cloned.1.call-start = ((), (), s32[]{:S(2)}) async-start(), calls=%async_computation.1 | async-start | bytes 524288 | tf_op jit(solution)/shard_map/psum | solution.py:19
  10.0 321.4 %all-gather.3.cloned.1.call-start = ((), (), s32[]{:S(2)}) async-start(), calls=%async_computation.2 | async-start | bytes 3342336 | tf_op jit(solution)/shard_map/all_gather | solution.py:36
  10.5 324.8 %reduce-scatter.4.cloned.1.call-start = ((), (), s32[]{:S(2)}) async-start(), calls=%async_computation.3 | async-start | bytes 3342336
  14.2 1.0 copy-start.3
  14.2 1.2 copy-start.4
  14.2 273.9 %copy-start.6 = (f32[192,16]{0,1:T(8,128)S(1)}, f32[192,16]{0,1:T(8,128)}, u32[]{:S(2)}) copy-start(f32[192,16]{0,1:T(8,128)} %param.12) | copy-start | bytes 36868
  14.2 273.9 %copy-start.7 = (f32[192,16]{0,1:T(8,128)S(1)}, f32[192,16]{0,1:T(8,128)}, u32[]{:S(2)}) copy-start(f32[192,16]{0,1:T(8,128)} %param.13) | copy-start | bytes 36868
  14.2 317.1 %copy-start.2 = (bf16[240,512]{1,0:T(8,128)(2,1)S(1)}, bf16[240,512]{1,0:T(8,128)(2,1)}, u32[]{:S(2)}) copy-start(bf16[240,512]{1,0:T(8,128)(2,1)} %param.8) | copy-start | bytes 737284
  15.7 321.5 %copy-start.1 = (bf16[1,192,512]{1,2,0:T(8,128)(2,1)S(1)}, bf16[1,192,512]{1,2,0:T(8,128)(2,1)}, u32[]{:S(2)}) copy-start(bf16[1,192,512]{1,2,0:T(8,128)(2,1)} %copy.34) | copy-start | bytes 589828
  289.5 0.6 copy-start.5
Sparse Core Ops, SparseCore 0:
  12.3 275.8 all-reduce.1
Sparse Core Ops, SparseCore 1:
  12.5 73.8 all-gather.2
  89.1 75.9 reduce-scatter.3
where the time goes:
time: 352 us
  waiting for transfers between devices  273 us (78%)
  blocking collectives  41.3 us (12%)
  between operations  15.6 us (4%)
  local copies, waits for them, and re-layouts  10.3 us (3%)
  matrix products  7.65 us (2%)
  other arithmetic  3.73 us (1%)
    psum x1, waiting for transfers between devices, body(): lax.psum(weights.astype(jnp.bfloat16), 'replica').astype(jnp.float32)  273 us
    all_gather x1, blocking collectives, body(): full_anchor = lax.all_gather(new_anchor, 'replica', axis=1, tiled=True)  41.3 us
    unnamed x23, local copies, waits for them, and re-layouts  10.3 us
  transfers between devices with their start and end apart: 3, of which 1 were waited for; matrix products, arithmetic and copies ran while one was open for 3% of the time, Pallas kernels for 0%

commit v1 on v0

v1 whole, which is shorter than its diff:
```python
import jax
import jax.numpy as jnp
from jax import lax
from jax.experimental import pallas as pl
from jax.experimental.pallas import tpu as pltpu
from jax.sharding import PartitionSpec as P

beta_one = 0.9
beta_two = 0.95
adam_eps = 1e-08
learn_rate = 0.0003
decay_rate = 0.1
outer_rate = 0.7
outer_mu = 0.9
blend_keep = 0.5

MESH = pl.DeviceIdType.MESH
NY = 8
NZ = 8
TOK = 240
D = 3072
KV = 512
ROWS = 192
PAIR = 2 * ROWS
NPAIR = NY // 2
AG_SUBS = 2
RS_SUBS = 2
SHARE = 16
F32 = jnp.float32
BF16 = jnp.bfloat16


def mod(value, size):
    return lax.rem(value + size, size)


def dot(a, b, dims):
    return lax.dot_general(a, b, (dims, ((), ())), preferred_element_type=F32)


def step_kernel(
    x_ref, c_ref, w_ref, m1_ref, m2_ref, a_ref, om_ref,
    ig_own, ig_recv, nw_ref, nf_ref, ns_ref, na_ref, nm_ref,
    xo, xp, cm, cp, wf, part, sb0, sb, rb0, rb, igs, wt, r1, s1, r2, fa, an, om, m1, m2,
    local_sem, xs, xr, ag_s, ag_r, rs_s, rs_r, z1_s, z1_r, g2_s, g2_r, g3_s, g3_r, z4_s, z4_r,
):
    rep = lax.axis_index("replica")
    fs = lax.axis_index("fsdp")
    half, y = fs // NY, lax.rem(fs, NY)
    xh, z, core = rep // (NZ * 2), lax.rem(rep // 2, NZ), lax.rem(rep, 2)

    def rep_of(xh_, z_, core_):
        return (xh_ * NZ + z_) * 2 + core_

    partner = (rep, (1 - half) * NY + y)
    ring = ((rep, half * NY + mod(y + 1, NY)), (rep, half * NY + mod(y - 1, NY)))
    zs = [(rep_of(xh, mod(z + d, NZ), core), fs) for d in range(1, NZ)]
    group = [(rep_of(lax.rem(xh + j // 2, 2), z, lax.rem(core + j % 2, 2)), fs) for j in range(1, 4)]

    barrier = pltpu.get_barrier_semaphore()
    for peer in (partner, *ring, *zs, *group):
        pl.semaphore_signal(barrier, inc=1, device_id=peer, device_id_type=MESH)

    def remote(src, dst, send, recv, peer):
        return pltpu.make_async_remote_copy(src, dst, send, recv, device_id=peer, device_id_type=MESH)

    quad = y // 2
    odd = lax.rem(y, 2)
    order = [mod(quad + 2, NPAIR), mod(quad + 1 + 2 * odd, NPAIR), mod(quad + 3 + 2 * odd, NPAIR), quad]

    def pair_columns(which, pair):
        return pl.ds(pl.multiple_of(which * (D // 2) + pair * PAIR, 128), PAIR)

    def block(ref, b, rows):
        start = pl.multiple_of(lax.rem(b, 2) * ROWS + rows[0], 16)
        return ref.at[b // 2, pl.ds(start, rows[1])]

    load_w = pltpu.make_async_copy(w_ref, block(wf, y, (0, ROWS)), local_sem.at[0])
    load_c = pltpu.make_async_copy(c_ref, cm, local_sem.at[1])
    load_w.start()
    load_c.start()
    load_x = [
        pltpu.make_async_copy(x_ref.at[:, pair_columns(half, order[i])], xo.at[order[i]], local_sem.at[2 + i])
        for i in range(NPAIR)
    ]
    loads = [
        pltpu.make_async_copy(src, dst, local_sem.at[2 + NPAIR + i])
        for i, (src, dst) in enumerate(((a_ref, an), (om_ref, om), (m1_ref, m1), (m2_ref, m2)))
    ]
    for load in (*load_x, *loads):
        load.start()
    load_w.wait()
    eye = (
        lax.broadcasted_iota(jnp.int32, (KV, KV), 0) == lax.broadcasted_iota(jnp.int32, (KV, KV), 1)
    ).astype(BF16)
    own_w = block(wf, y, (0, ROWS))[...]
    wt[...] = dot(eye, own_w, ((1,), (1,))).astype(BF16).reshape(2, NZ, 2 * SHARE, ROWS)
    load_c.wait()
    pl.semaphore_wait(barrier, 3 + len(zs) + len(group))

    send_c = remote(cm, cp, xs.at[0], xr.at[0], partner)
    send_x = [
        remote(x_ref.at[:, pair_columns(1 - half, order[i])], xp.at[order[i]], xs.at[1 + i], xr.at[1 + i], partner)
        for i in range(NPAIR)
    ]
    send_ig = [
        remote(igs.at[i], ig_recv.at[i], xs.at[1 + NPAIR + i], xr.at[1 + NPAIR + i], partner) for i in range(NPAIR)
    ]

    sub = ROWS // AG_SUBS

    def ag(d, s, j):
        place = block(wf, mod(y - s, NY) if d == 0 else mod(y + s, NY), (j * sub, sub))
        return remote(place, place, ag_s.at[d, s, j], ag_r.at[d, s, j], ring[d])

    def ag_subs(d, s):
        if s < NY // 2 - 1:
            return range(AG_SUBS)
        return range(AG_SUBS // 2) if d == 0 else range(AG_SUBS // 2, AG_SUBS)

    send_c.start()
    for j in range(AG_SUBS):
        for d in range(2):
            ag(d, 0, j).start()
    for copy in send_x:
        copy.start()
    z1 = [
        remote(wt.at[:, mod(z + d, NZ)], r1.at[d - 1], z1_s.at[d - 1], z1_r.at[d - 1], zs[d - 1]) for d in range(1, NZ)
    ]
    for copy in z1:
        copy.start()

    def ag_forward(s):
        for j in range(AG_SUBS):
            for d in range(2):
                if j in ag_subs(d, s - 1):
                    ag(d, s - 1, j).wait_recv()
                if s < NY // 2 and j in ag_subs(d, s):
                    ag(d, s, j).start()

    rsub = ROWS // RS_SUBS

    def rs(d, s, j):
        rows = pl.ds(j * rsub, rsub)
        if s == 0:
            return remote(sb0.at[d, rows], rb0.at[d, rows], rs_s.at[d, s, j], rs_r.at[d, s, j], ring[d])
        return remote(sb.at[d, s - 1, rows], rb.at[d, s - 1, rows], rs_s.at[d, s, j], rs_r.at[d, s, j], ring[d])

    def rs_step(s):
        for j in range(RS_SUBS):
            rows = pl.ds(j * rsub, rsub)
            for d in range(2):
                dest = mod(y + 4 - s, NY) if d == 0 else mod(y - 4 + s, NY)
                own = block(part, dest, (j * rsub, rsub))
                near = pl.ds(d * (KV // 2), KV // 2)
                far = pl.ds((1 - d) * (KV // 2), KV // 2)
                if s == 0:
                    sb0[d, rows] = own[:, near].astype(BF16)
                elif s == 1:
                    rs(d, 0, j).wait_recv()
                    sb[d, 0, rows, near] = (own[:, near] + rb0[d, rows].astype(F32)).astype(BF16)
                    sb[d, 0, rows, far] = own[:, far].astype(BF16)
                else:
                    rs(d, s - 1, j).wait_recv()
                    sb[d, s - 1, rows] = (own[...] + rb[d, s - 2, rows].astype(F32)).astype(BF16)
                rs(d, s, j).start()

    def make_part(i):
        load_x[i].wait()
        send_x[i].wait_recv()
        part[order[i]] = dot(xo[order[i]], cm[...], ((0,), (0,))) + dot(xp[order[i]], cp[...], ((0,), (0,)))

    ag_forward(1)

    for copy in z1:
        copy.wait_recv()
    total = wt[:, pl.ds(z, 1)].astype(F32).reshape(2, 2 * SHARE, ROWS)
    for d in range(NZ - 1):
        total = total + r1[d].astype(F32)
    s1[...] = total.reshape(2, 2, SHARE, ROWS)
    g2 = [
        remote(
            s1.at[lax.rem(xh + j // 2, 2), lax.rem(core + j % 2, 2)], r2.at[j - 1],
            g2_s.at[j - 1], g2_r.at[j - 1], group[j - 1],
        )
        for j in range(1, 4)
    ]
    for copy in g2:
        copy.start()

    ag_forward(2)
    send_c.wait_recv()
    make_part(0)
    rs_step(0)

    for copy in g2:
        copy.wait_recv()
    for load in loads[:2]:
        load.wait()
    share = s1[pl.ds(xh, 1), pl.ds(core, 1)].reshape(SHARE, ROWS)
    share = share + r2[0] + r2[1] + r2[2]
    anchor = an[...]
    delta = anchor - share / (2 * NZ * 2)
    new_momentum = outer_mu * om[...] + delta
    new_anchor = anchor - outer_rate * (delta + outer_mu * new_momentum)
    nm_ref[...] = new_momentum
    na_ref[...] = new_anchor
    fa[pl.ds(xh, 1), pl.ds(z, 1), pl.ds(core, 1)] = new_anchor[None, None, None]
    mine = fa.at[xh, z, core]
    g3 = [remote(mine, mine, g3_s.at[j], g3_r.at[j], group[j]) for j in range(3)]
    for copy in g3:
        copy.start()

    ag_forward(3)
    make_part(1)
    rs_step(1)
    for copy in g3:
        copy.wait_recv()
    layer = fa.at[:, z]
    z4 = [remote(layer, layer, z4_s.at[d], z4_r.at[d], zs[d]) for d in range(NZ - 1)]
    for copy in z4:
        copy.start()

    ag_forward(4)
    for i in range(NPAIR):
        igs[i] = dot(cp[...], wf[i], ((1,), (1,))).astype(BF16)
        send_ig[i].start()

    make_part(2)
    rs_step(2)
    make_part(3)
    rs_step(3)
    for i in range(NPAIR):
        ig_own[i] = dot(cm[...], wf[i], ((1,), (1,))).astype(BF16)

    for load in loads[2:]:
        load.wait()
    for copy in z4:
        copy.wait_recv()
    full_anchor = fa[...].reshape(KV, ROWS).T
    for j in range(RS_SUBS):
        rows = pl.ds(j * rsub, rsub)
        for d in range(2):
            rs(d, 3, j).wait_recv()
        gradient = block(part, y, (j * rsub, rsub))[...] + rb[0, 2, rows].astype(F32) + rb[1, 2, rows].astype(F32)
        new_first = beta_one * m1[rows] + (1.0 - beta_one) * gradient
        new_second = beta_two * m2[rows] + (1.0 - beta_two) * gradient * gradient
        nf_ref[rows] = new_first
        ns_ref[rows] = new_second
        weights = block(wf, y, (j * rsub, rsub))[...].astype(F32)
        update = new_first / (jnp.sqrt(new_second) + adam_eps)
        inner = weights - learn_rate * (update + decay_rate * weights)
        blend = blend_keep * inner + (1.0 - blend_keep) * full_anchor[j * rsub : (j + 1) * rsub]
        nw_ref[rows] = blend.astype(BF16)

    for copy in send_ig:
        copy.wait_recv()
    for copy in (send_c, *send_x, *send_ig, *z1, *g2, *g3, *z4):
        copy.wait_send()
    for s in range(NY // 2):
        for d in range(2):
            for j in ag_subs(d, s):
                ag(d, s, j).wait_send()
            for j in range(RS_SUBS):
                rs(d, s, j).wait_send()


def write_kernel(half_ref, ig_own, ig_recv, nw, nf, ns, na, nm, o_ig, o_nw, o_nf, o_ns, o_na, o_nm, sem):
    half = half_ref[0]
    copies = []
    for i in range(NPAIR):
        for which, source in ((half, ig_own), (1 - half, ig_recv)):
            columns = pl.ds(pl.multiple_of(which * (D // 2) + i * PAIR, 128), PAIR)
            copies.append((source.at[i], o_ig.at[:, columns]))
    copies += [(nw, o_nw), (nf, o_nf), (ns, o_ns), (na, o_na), (nm, o_nm)]
    copies = [pltpu.make_async_copy(src, dst, sem.at[k]) for k, (src, dst) in enumerate(copies)]
    for copy in copies:
        copy.start()
    for copy in copies:
        copy.wait()


def body(layer_input, cotangent, local_weight, first_moment, second_moment, anchor, outer_momentum):
    vmem = pl.BlockSpec(memory_space=pltpu.VMEM)
    hbm = pl.BlockSpec(memory_space=pl.ANY)
    shape = jax.ShapeDtypeStruct
    dma = pltpu.SemaphoreType.DMA
    small = shape((SHARE, ROWS), F32)
    wide = shape((ROWS, KV), F32)
    results = pl.pallas_call(
        step_kernel,
        out_shape=(
            shape((NPAIR, TOK, PAIR), BF16), shape((NPAIR, TOK, PAIR), BF16),
            shape((ROWS, KV), BF16), wide, wide, small, small,
        ),
        in_specs=[hbm] * 7,
        out_specs=[vmem] * 7,
        scratch_shapes=[
            pltpu.VMEM((NPAIR, TOK, PAIR), BF16),
            pltpu.VMEM((NPAIR, TOK, PAIR), BF16),
            pltpu.VMEM((TOK, KV), BF16),
            pltpu.VMEM((TOK, KV), BF16),
            pltpu.VMEM((NPAIR, PAIR, KV), BF16),
            pltpu.VMEM((NPAIR, PAIR, KV), F32),
            pltpu.VMEM((2, ROWS, KV // 2), BF16),
            pltpu.VMEM((2, 3, ROWS, KV), BF16),
            pltpu.VMEM((2, ROWS, KV // 2), BF16),
            pltpu.VMEM((2, 3, ROWS, KV), BF16),
            pltpu.VMEM((NPAIR, TOK, PAIR), BF16),
            pltpu.VMEM((2, NZ, 2 * SHARE, ROWS), BF16),
            pltpu.VMEM((NZ - 1, 2, 2 * SHARE, ROWS), BF16),
            pltpu.VMEM((2, 2, SHARE, ROWS), F32),
            pltpu.VMEM((3, SHARE, ROWS), F32),
            pltpu.VMEM((2, NZ, 2, SHARE, ROWS), F32),
            pltpu.VMEM((SHARE, ROWS), F32),
            pltpu.VMEM((SHARE, ROWS), F32),
            pltpu.VMEM((ROWS, KV), F32),
            pltpu.VMEM((ROWS, KV), F32),
            dma((2 + NPAIR + 4,)),
            dma((1 + 2 * NPAIR,)), dma((1 + 2 * NPAIR,)),
            dma((2, NY // 2, AG_SUBS)), dma((2, NY // 2, AG_SUBS)),
            dma((2, NY // 2, RS_SUBS)), dma((2, NY // 2, RS_SUBS)),
            dma((NZ - 1,)), dma((NZ - 1,)),
            dma((3,)), dma((3,)),
            dma((3,)), dma((3,)),
            dma((NZ - 1,)), dma((NZ - 1,)),
        ],
        compiler_params=pltpu.CompilerParams(
            collective_id=0, has_side_effects=True, vmem_limit_bytes=40 << 20
        ),
        cost_estimate=pl.CostEstimate(flops=1_600_000_000, bytes_accessed=5_000_000, transcendentals=200_000),
        name="step",
    )(
        layer_input, cotangent, local_weight[0], first_moment[0], second_moment[0], anchor.T, outer_momentum.T
    )
    half = (lax.axis_index("fsdp") // NY).astype(jnp.int32).reshape(1)
    outs = pl.pallas_call(
        write_kernel,
        out_shape=(shape((TOK, D), BF16), shape((ROWS, KV), BF16), wide, wide, small, small),
        in_specs=[pl.BlockSpec(memory_space=pltpu.SMEM)] + [vmem] * 7,
        out_specs=[hbm] * 6,
        scratch_shapes=[dma((2 * NPAIR + 5,))],
        name="write",
    )(half, *results)
    input_grad, new_weight, new_first, new_second, new_anchor, new_momentum = outs
    return input_grad, new_weight[None], new_first[None], new_second[None], new_anchor.T, new_momentum.T


def solution(mesh):
    in_specs = (
        P(("replica", "fsdp"), None),
        P(("replica", "fsdp"), None),
        P("replica", "fsdp", None),
        P("replica", "fsdp", None),
        P("replica", "fsdp", None),
        P("fsdp", "replica"),
        P("fsdp", "replica"),
    )
    out_specs = (
        P(("replica", "fsdp"), None),
        P("replica", "fsdp", None),
        P("replica", "fsdp", None),
        P("replica", "fsdp", None),
        P("fsdp", "replica"),
        P("fsdp", "replica"),
    )
    return jax.shard_map(body, mesh=mesh, in_specs=in_specs, out_specs=out_specs, check_vma=False)
```

time: 352 us -> 76 us (0.22)
  waiting for transfers between devices: 273 us -> 0 us
  Pallas kernels: 0 us -> 62.6 us
  blocking collectives: 41.3 us -> 0 us
  between operations: 15.6 us -> 0.69 us
  matrix products: 7.65 us -> 0 us
  other arithmetic: 3.73 us -> 0 us
    psum x1 -> x0, waiting for transfers between devices: 273 us -> none  [body(): lax.psum(weights.astype(jnp.bfloat16), 'replica').astype(jnp.float32)]
    pallas_call x0 -> x2, Pallas kernels: none -> 62.6 us  [the longest x1 59.4 us: body(): pl.pallas_call(step_kernel, out_shape=(shape((NPAIR, TOK, PAIR), BF16), s...]
    all_gather x1 -> x0, blocking collectives: 41.3 us -> none  [body(): full_anchor = lax.all_gather(new_anchor, 'replica', axis=1, tiled=True)]
    dot_general x2 -> x0, matrix products: 7.65 us -> none  [the longest x1 4.01 us: body(): lax.dot_general(cotangent, lax.all_gather(weight_rows, 'fsdp', axis=0, ti...]
    unnamed x23 -> x28, local copies, waits for them, and re-layouts: 10.3 us -> 11.8 us
  transfers between devices with their start and end apart: 3 -> 0, of which waited for: 1 -> 0; matrix products, arithmetic and copies ran while one was open for 3% -> 0% of each run, Pallas kernels for 0% -> 0%
where the time goes in v1:
time: 76 us; the launch traced here: 75 us
  Pallas kernels  62.6 us (82%)
  local copies, waits for them, and re-layouts  11.8 us (16%)
    pallas_call x1, Pallas kernels, body(): pl.pallas_call(step_kernel, out_shape=(shape((NPAIR, TOK, PAIR), BF16), s...  59.4 us
    unnamed x28, local copies, waits for them, and re-layouts  11.8 us
    pallas_call x1, Pallas kernels, body(): pl.pallas_call(write_kernel, out_shape=(shape((TOK, D), BF16), shape((ROW...  3.18 us

profile of v1, /device:TPU:1, one launch (start us, length us, event | category | flops | bytes accessed | tf_op | source)
XLA Modules:
  0.0 75.0 jit_solution(2661706261180731961)
XLA Ops:
  0.6 0.0 copy-start.7
  0.7 1.4 %copy-done.7 = bf16[240,3072]{1,0:T(8,128)(2,1)S(1)} copy-done((bf16[240,3072]{1,0:T(8,128)(2,1)S(1)}, bf16[240,3072]{1,0:T(8,128)(2,1)}, u32[]{:S(2)}) %copy-start.7) | copy-done | bytes 1474584
  2.0 0.0 copy-start.8
  2.0 1.0 %copy-done.8 = f32[1,192,512]{2,1,0:T(8,128)S(1)} copy-done((f32[1,192,512]{2,1,0:T(8,128)S(1)}, f32[1,192,512]{2,1,0:T(8,128)}, u32[]{:S(2)}) %copy-start.8) | copy-done | bytes 393240
  3.0 0.0 copy-start.9
  3.0 1.0 %copy-done.9 = f32[1,192,512]{2,1,0:T(8,128)S(1)} copy-done((f32[1,192,512]{2,1,0:T(8,128)S(1)}, f32[1,192,512]{2,1,0:T(8,128)}, u32[]{:S(2)}) %copy-start.9) | copy-done | bytes 393240
  4.0 0.0 copy-start.10
  4.0 0.9 %copy-done.10 = bf16[240,512]{1,0:T(8,128)(2,1)S(1)} copy-done((bf16[240,512]{1,0:T(8,128)(2,1)S(1)}, bf16[240,512]{1,0:T(8,128)(2,1)}, u32[]{:S(2)}) %copy-start.10) | copy-done | bytes 245784
  5.0 0.0 copy-start.11
  5.0 0.9 %copy-done.11 = bf16[1,192,512]{2,1,0:T(8,128)(2,1)S(1)} copy-done((bf16[1,192,512]{2,1,0:T(8,128)(2,1)S(1)}, bf16[1,192,512]{2,1,0:T(8,128)(2,1)}, u32[]{:S(2)}) %copy-start.11) | copy-done | bytes 196632
  5.9 0.0 copy-start.12
  5.9 0.7 copy-done.12
  6.6 0.0 copy-start.13
  6.6 0.7 copy-done.13
  7.3 59.4 %step.1 = (bf16[4,240,384]{2,1,0:T(8,128)(2,1)S(1)}, bf16[4,240,384]{2,1,0:T(8,128)(2,1)S(1)}, bf16[192,512]{1,0:T(8,128)(2,1)S(1)}, f32[192,512]{1,0:T(8,128)S(...) custom-call(bf16[240,3072]{1,0:T(8,128)(2,1)S(1)} %copy-done.7, ...), custom_call_target="tpu_custom_call" | custom-call | flops 1600000000 | bytes 5000000 | tf_op jit(solution)/shard_map/step/pallas_call | solution.py:290
  66.7 0.0 copy-start
  66.7 0.9 %copy-done = bf16[4,240,384]{2,1,0:T(8,128)(2,1)} copy-done((bf16[4,240,384]{2,1,0:T(8,128)(2,1)}, bf16[4,240,384]{2,1,0:T(8,128)(2,1)S(1)}, u32[]{:S(2)}) %copy-start) | copy-done | bytes 737304
  67.6 0.0 copy-start.1
  67.6 0.9 %copy-done.1 = bf16[4,240,384]{2,1,0:T(8,128)(2,1)} copy-done((bf16[4,240,384]{2,1,0:T(8,128)(2,1)}, bf16[4,240,384]{2,1,0:T(8,128)(2,1)S(1)}, u32[]{:S(2)}) %copy-start.1) | copy-done | bytes 737304
  68.5 0.0 copy-start.2
  68.5 0.7 copy-done.2
  69.2 0.0 copy-start.3
  69.2 0.7 copy-done.3
  70.0 0.0 copy-start.4
  70.0 0.7 copy-done.4
  70.7 0.0 copy-start.5
  70.7 0.6 copy-done.5
  71.3 0.0 copy-start.6
  71.3 0.6 copy-done.6
  71.9 3.2 %write.1 = (bf16[240,3072]{1,0:T(8,128)(2,1)}, bf16[192,512]{1,0:T(8,128)(2,1)}, f32[192,512]{1,0:T(8,128)}, f32[192,512]{1,0:T(8,128)}, f32[16,192]{1,0:T(8,128)}, /*index=5*/f32[16,192]{1,0:T(8,128)}) custom-call(s32[1]{0:T(128)} %bitcast.half_ref, bf16[4,240,384]{2,1,0:T(8,128)(2,1)} %copy-done, bf16[4,240,384]{2,1,0:T(8,128)(2,1)} %copy-done.1, ...), custom_call_target="tpu_custom_call" | custom-call | tf_op jit(solution)/shard_map/write/pallas_call | solution.py:337
Async XLA Ops:
  0.6 1.4 %copy-start.7 = (bf16[240,3072]{1,0:T(8,128)(2,1)S(1)}, bf16[240,3072]{1,0:T(8,128)(2,1)}, u32[]{:S(2)}) copy-start(bf16[240,3072]{1,0:T(8,128)(2,1)} %x_ref.1) | copy-start | bytes 4423684
  2.0 1.0 %copy-start.8 = (f32[1,192,512]{2,1,0:T(8,128)S(1)}, f32[1,192,512]{2,1,0:T(8,128)}, u32[]{:S(2)}) copy-start(f32[1,192,512]{2,1,0:T(8,128)} %param.10) | copy-start | bytes 1179652
  3.0 1.0 %copy-start.9 = (f32[1,192,512]{2,1,0:T(8,128)S(1)}, f32[1,192,512]{2,1,0:T(8,128)}, u32[]{:S(2)}) copy-start(f32[1,192,512]{2,1,0:T(8,128)} %param.11) | copy-start | bytes 1179652
  4.0 0.9 %copy-start.10 = (bf16[240,512]{1,0:T(8,128)(2,1)S(1)}, bf16[240,512]{1,0:T(8,128)(2,1)}, u32[]{:S(2)}) copy-start(bf16[240,512]{1,0:T(8,128)(2,1)} %c_ref.1) | copy-start | bytes 737284
  5.0 0.9 %copy-start.11 = (bf16[1,192,512]{2,1,0:T(8,128)(2,1)S(1)}, bf16[1,192,512]{2,1,0:T(8,128)(2,1)}, u32[]{:S(2)}) copy-start(bf16[1,192,512]{2,1,0:T(8,128)(2,1)} %param.9) | copy-start | bytes 589828
  5.9 0.7 copy-start.12
  6.6 0.7 copy-start.13
  66.7 0.9 %copy-start = (bf16[4,240,384]{2,1,0:T(8,128)(2,1)}, bf16[4,240,384]{2,1,0:T(8,128)(2,1)S(1)}, u32[]{:S(2)}) copy-start(bf16[4,240,384]{2,1,0:T(8,128)(2,1)S(1)} %get-tuple-element.19.ig_own) | copy-start | bytes 2211844
  67.6 0.9 %copy-start.1 = (bf16[4,240,384]{2,1,0:T(8,128)(2,1)}, bf16[4,240,384]{2,1,0:T(8,128)(2,1)S(1)}, u32[]{:S(2)}) copy-start(bf16[4,240,384]{2,1,0:T(8,128)(2,1)S(1)} %get-tuple-element.20.ig_recv) | copy-start | bytes 2211844
  68.5 0.7 copy-start.2
  69.2 0.8 %copy-start.3 = (f32[192,512]{1,0:T(8,128)}, f32[192,512]{1,0:T(8,128)S(1)}, u32[]{:S(2)}) copy-start(f32[192,512]{1,0:T(8,128)S(1)} %get-tuple-element.23.ns) | copy-start | bytes 1179652
  70.0 0.7 copy-start.4
  70.7 0.6 copy-start.5
  71.3 0.6 copy-start.6

commit v2 on v1

--- a/solution.py
+++ b/solution.py
@@ -25,6 +25,8 @@
 NPAIR = NY // 2
 AG_SUBS = 2
 RS_SUBS = 2
+MID = 128
+SIDE = PAIR - MID
 SHARE = 16
 F32 = jnp.float32
 BF16 = jnp.bfloat16
@@ -40,9 +42,9 @@
 
 def step_kernel(
     x_ref, c_ref, w_ref, m1_ref, m2_ref, a_ref, om_ref,
-    ig_own, ig_recv, nw_ref, nf_ref, ns_ref, na_ref, nm_ref,
-    xo, xp, cm, cp, wf, part, sb0, sb, rb0, rb, igs, wt, r1, s1, r2, fa, an, om, m1, m2,
-    local_sem, xs, xr, ag_s, ag_r, rs_s, rs_r, z1_s, z1_r, g2_s, g2_r, g3_s, g3_r, z4_s, z4_r,
+    ig_own, ig_recv, ig_mid, nw_ref, nf_ref, ns_ref, na_ref, nm_ref,
+    xo, xp, cm, cp, wf, wo, part, sb0, sb, rb0, rb, igs, wt, r1, s1, r2, fa, an, om, m1, m2,
+    local_sem, xs, xr, ag_s, ag_r, mid_s, mid_r, rs_s, rs_r, z1_s, z1_r, g2_s, g2_r, g3_s, g3_r, z4_s, z4_r,
 ):
     rep = lax.axis_index("replica")
     fs = lax.axis_index("fsdp")
@@ -118,12 +120,31 @@
             return range(AG_SUBS)
         return range(AG_SUBS // 2) if d == 0 else range(AG_SUBS // 2, AG_SUBS)
 
+    middle = pl.ds(pl.multiple_of(MID // 2 * odd, 16), MID // 2)
+    send_mid = remote(
+        wf.at[quad, pl.ds(pl.multiple_of(MID + MID // 2 * odd, 16), MID // 2)], wo.at[quad, middle],
+        xs.at[1 + 2 * NPAIR], xr.at[1 + 2 * NPAIR], partner,
+    )
+
+    def mid(d, s):
+        b = mod(y - s, NY) if d == 0 else mod(y + s, NY)
+        start, size = (0, MID // 2) if s < NY // 2 - 1 else (d * (MID // 4), MID // 4)
+        place = wo.at[b // 2, pl.ds(pl.multiple_of(lax.rem(b, 2) * (MID // 2) + start, 16), size)]
+        return remote(place, place, mid_s.at[d, s], mid_r.at[d, s], ring[d])
+
+    def mid_forward(s):
+        for d in range(2):
+            if s > 0:
+                mid(d, s - 1).wait_recv()
+            if s < NY // 2:
+                mid(d, s).start()
+
+    send_mid.start()
     send_c.start()
     for j in range(AG_SUBS):
         for d in range(2):
             ag(d, 0, j).start()
-    for copy in send_x:
-        copy.start()
+    send_x[0].start()
     z1 = [
         remote(wt.at[:, mod(z + d, NZ)], r1.at[d - 1], z1_s.at[d - 1], z1_r.at[d - 1], zs[d - 1]) for d in range(1, NZ)
     ]
@@ -171,6 +192,8 @@
         part[order[i]] = dot(xo[order[i]], cm[...], ((0,), (0,))) + dot(xp[order[i]], cp[...], ((0,), (0,)))
 
     ag_forward(1)
+    send_mid.wait_recv()
+    mid_forward(0)
 
     for copy in z1:
         copy.wait_recv()
@@ -187,11 +210,14 @@
     ]
     for copy in g2:
         copy.start()
+    send_x[1].start()
 
     ag_forward(2)
+    mid_forward(1)
     send_c.wait_recv()
     make_part(0)
     rs_step(0)
+    send_x[2].start()
 
     for copy in g2:
         copy.wait_recv()
@@ -210,8 +236,10 @@
     g3 = [remote(mine, mine, g3_s.at[j], g3_r.at[j], group[j]) for j in range(3)]
     for copy in g3:
         copy.start()
+    send_x[3].start()
 
     ag_forward(3)
+    mid_forward(2)
     make_part(1)
     rs_step(1)
     for copy in g3:
@@ -222,8 +250,10 @@
         copy.start()
 
     ag_forward(4)
+    mid_forward(3)
     for i in range(NPAIR):
-        igs[i] = dot(cp[...], wf[i], ((1,), (1,))).astype(BF16)
+        for k, rows in enumerate((pl.ds(0, SIDE // 2), pl.ds(PAIR - SIDE // 2, SIDE // 2))):
+            igs[i, :, k * (SIDE // 2) : (k + 1) * (SIDE // 2)] = dot(cp[...], wf[i, rows], ((1,), (1,))).astype(BF16)
         send_ig[i].start()
 
     make_part(2)
@@ -232,6 +262,9 @@
     rs_step(3)
     for i in range(NPAIR):
         ig_own[i] = dot(cm[...], wf[i], ((1,), (1,))).astype(BF16)
+    mid_forward(4)
+    for i in range(NPAIR):
+        ig_mid[i] = dot(cm[...], wo[i], ((1,), (1,))).astype(BF16)
 
     for load in loads[2:]:
         load.wait()
@@ -255,23 +288,29 @@
 
     for copy in send_ig:
         copy.wait_recv()
-    for copy in (send_c, *send_x, *send_ig, *z1, *g2, *g3, *z4):
+    for copy in (send_mid, send_c, *send_x, *send_ig, *z1, *g2, *g3, *z4):
         copy.wait_send()
     for s in range(NY // 2):
         for d in range(2):
+            mid(d, s).wait_send()
             for j in ag_subs(d, s):
                 ag(d, s, j).wait_send()
             for j in range(RS_SUBS):
                 rs(d, s, j).wait_send()
 
 
-def write_kernel(half_ref, ig_own, ig_recv, nw, nf, ns, na, nm, o_ig, o_nw, o_nf, o_ns, o_na, o_nm, sem):
+def write_kernel(half_ref, ig_own, ig_recv, ig_mid, nw, nf, ns, na, nm, o_ig, o_nw, o_nf, o_ns, o_na, o_nm, sem):
     half = half_ref[0]
     copies = []
     for i in range(NPAIR):
-        for which, source in ((half, ig_own), (1 - half, ig_recv)):
-            columns = pl.ds(pl.multiple_of(which * (D // 2) + i * PAIR, 128), PAIR)
-            copies.append((source.at[i], o_ig.at[:, columns]))
+        for which, source, start, size in (
+            (half, ig_own.at[i], 0, PAIR),
+            (1 - half, ig_recv.at[i, :, pl.ds(0, SIDE // 2)], 0, SIDE // 2),
+            (1 - half, ig_mid.at[i], SIDE // 2, MID),
+            (1 - half, ig_recv.at[i, :, pl.ds(SIDE // 2, SIDE // 2)], SIDE // 2 + MID, SIDE // 2),
+        ):
+            columns = pl.ds(pl.multiple_of(which * (D // 2) + i * PAIR + start, 128), size)
+            copies.append((source, o_ig.at[:, columns]))
     copies += [(nw, o_nw), (nf, o_nf), (ns, o_ns), (na, o_na), (nm, o_nm)]
     copies = [pltpu.make_async_copy(src, dst, sem.at[k]) for k, (src, dst) in enumerate(copies)]
     for copy in copies:
@@ -290,23 +329,24 @@
     results = pl.pallas_call(
         step_kernel,
         out_shape=(
-            shape((NPAIR, TOK, PAIR), BF16), shape((NPAIR, TOK, PAIR), BF16),
+            shape((NPAIR, TOK, PAIR), BF16), shape((NPAIR, TOK, SIDE), BF16), shape((NPAIR, TOK, MID), BF16),
             shape((ROWS, KV), BF16), wide, wide, small, small,
         ),
         in_specs=[hbm] * 7,
-        out_specs=[vmem] * 7,
+        out_specs=[vmem] * 8,
         scratch_shapes=[
             pltpu.VMEM((NPAIR, TOK, PAIR), BF16),
             pltpu.VMEM((NPAIR, TOK, PAIR), BF16),
             pltpu.VMEM((TOK, KV), BF16),
             pltpu.VMEM((TOK, KV), BF16),
             pltpu.VMEM((NPAIR, PAIR, KV), BF16),
+            pltpu.VMEM((NPAIR, MID, KV), BF16),
             pltpu.VMEM((NPAIR, PAIR, KV), F32),
             pltpu.VMEM((2, ROWS, KV // 2), BF16),
             pltpu.VMEM((2, 3, ROWS, KV), BF16),
             pltpu.VMEM((2, ROWS, KV // 2), BF16),
             pltpu.VMEM((2, 3, ROWS, KV), BF16),
-            pltpu.VMEM((NPAIR, TOK, PAIR), BF16),
+            pltpu.VMEM((NPAIR, TOK, SIDE), BF16),
             pltpu.VMEM((2, NZ, 2 * SHARE, ROWS), BF16),
             pltpu.VMEM((NZ - 1, 2, 2 * SHARE, ROWS), BF16),
             pltpu.VMEM((2, 2, SHARE, ROWS), F32),
@@ -317,8 +357,9 @@
             pltpu.VMEM((ROWS, KV), F32),
             pltpu.VMEM((ROWS, KV), F32),
             dma((2 + NPAIR + 4,)),
-            dma((1 + 2 * NPAIR,)), dma((1 + 2 * NPAIR,)),
+            dma((2 + 2 * NPAIR,)), dma((2 + 2 * NPAIR,)),
             dma((2, NY // 2, AG_SUBS)), dma((2, NY // 2, AG_SUBS)),
+            dma((2, NY // 2)), dma((2, NY // 2)),
             dma((2, NY // 2, RS_SUBS)), dma((2, NY // 2, RS_SUBS)),
             dma((NZ - 1,)), dma((NZ - 1,)),
             dma((3,)), dma((3,)),
@@ -331,17 +372,22 @@
         cost_estimate=pl.CostEstimate(flops=1_600_000_000, bytes_accessed=5_000_000, transcendentals=200_000),
         name="step",
     )(
-        layer_input, cotangent, local_weight[0], first_moment[0], second_moment[0], anchor.T, outer_momentum.T
+        *(
+            pltpu.with_memory_space_constraint(array, pltpu.HBM)
+            for array in (
+                layer_input, cotangent, local_weight[0], first_moment[0], second_moment[0], anchor.T, outer_momentum.T
+            )
+        )
     )
     half = (lax.axis_index("fsdp") // NY).astype(jnp.int32).reshape(1)
     outs = pl.pallas_call(
         write_kernel,
         out_shape=(shape((TOK, D), BF16), shape((ROWS, KV), BF16), wide, wide, small, small),
-        in_specs=[pl.BlockSpec(memory_space=pltpu.SMEM)] + [vmem] * 7,
+        in_specs=[pl.BlockSpec(memory_space=pltpu.SMEM)] + [vmem] * 8,
         out_specs=[hbm] * 6,
-        scratch_shapes=[dma((2 * NPAIR + 5,))],
+        scratch_shapes=[dma((4 * NPAIR + 5,))],
         name="write",
-    )(half, *results)
+    )(half, *(pltpu.with_memory_space_constraint(array, pltpu.VMEM) for array in results))
     input_grad, new_weight, new_first, new_second, new_anchor, new_momentum = outs
     return input_grad, new_weight[None], new_first[None], new_second[None], new_anchor.T, new_momentum.T
 

time: 76 us -> 53.6 us (0.71); the launches traced: 75 us -> 53.5 us
  local copies, waits for them, and re-layouts: 11.8 us -> 0 us
  Pallas kernels: 62.6 us -> 52.8 us
    unnamed x28 -> x0, local copies, waits for them, and re-layouts: 11.8 us -> none
    pallas_call x1, Pallas kernels: 59.4 us -> 51.2 us  [body(): pl.pallas_call(step_kernel, out_shape=(shape((NPAIR, TOK, PAIR), BF16), s...]
    pallas_call x1, Pallas kernels: 3.18 us -> 1.62 us  [body(): pl.pallas_call(write_kernel, out_shape=(shape((TOK, D), BF16), shape((ROW...]
where the time goes in v2:
time: 53.6 us; the launch traced here: 53.5 us
  Pallas kernels  52.8 us (99%)
  between operations  0.66 us (1%)
    pallas_call x1, Pallas kernels, body(): pl.pallas_call(step_kernel, out_shape=(shape((NPAIR, TOK, PAIR), BF16), s...  51.2 us
    pallas_call x1, Pallas kernels, body(): pl.pallas_call(write_kernel, out_shape=(shape((TOK, D), BF16), shape((ROW...  1.62 us

profile of v2, /device:TPU:1, one launch (start us, length us, event | category | flops | bytes accessed | tf_op | source)
XLA Modules:
  0.0 53.5 jit_solution(7083277338525233919)
XLA Ops:
  0.6 51.2 %step.1 = (bf16[4,240,384]{2,1,0:T(8,128)(2,1)S(1)}, bf16[4,240,256]{2,1,0:T(8,128)(2,1)S(1)}, bf16[4,240,128]{2,1,0:T(8,128)(2,1)S(1)}, bf16[192,512]{1,0:T(8,1...) custom-call(bf16[240,3072]{1,0:T(8,128)(2,1)} %x_ref.1, ...), custom_call_target="tpu_custom_call" | custom-call | flops 1600000000 | bytes 5000000 | tf_op jit(solution)/shard_map/step/pallas_call | solution.py:329
  51.8 1.6 %write.1 = (bf16[240,3072]{1,0:T(8,128)(2,1)}, bf16[192,512]{1,0:T(8,128)(2,1)}, f32[192,512]{1,0:T(8,128)}, f32[192,512]{1,0:T(8,128)}, f32[16,192]{1,0:T(8,128)}, /*index=5*/f32[16,192]{1,0:T(8,128)}) custom-call(s32[1]{0:T(128)} %bitcast.half_ref, bf16[4,240,384]{2,1,0:T(8,128)(2,1)S(1)} %get-tuple-element.20.ig_own, ...), custom_call_target="tpu_custom_call" | custom-call | tf_op jit(solution)/shard_map/write/pallas_call | solution.py:383

commit v3 on v2

--- a/solution.py
+++ b/solution.py
@@ -43,8 +43,8 @@
 def step_kernel(
     x_ref, c_ref, w_ref, m1_ref, m2_ref, a_ref, om_ref,
     ig_own, ig_recv, ig_mid, nw_ref, nf_ref, ns_ref, na_ref, nm_ref,
-    xo, xp, cm, cp, wf, wo, part, sb0, sb, rb0, rb, igs, wt, r1, s1, r2, fa, an, om, m1, m2,
-    local_sem, xs, xr, ag_s, ag_r, mid_s, mid_r, rs_s, rs_r, z1_s, z1_r, g2_s, g2_r, g3_s, g3_r, z4_s, z4_r,
+    xo, xp, cm, cp, wf, wo, part, sb0, sb, rb0, rb, igs, wt, r1, s1, r2, s2, r3, ao, aop, fa, m1, m2,
+    local_sem, xs, xr, ag_s, ag_r, mid_s, mid_r, rs_s, rs_r, z1_s, z1_r, z4_s, z4_r, g_s, g_r, hello, ready,
 ):
     rep = lax.axis_index("replica")
     fs = lax.axis_index("fsdp")
@@ -57,11 +57,20 @@
     partner = (rep, (1 - half) * NY + y)
     ring = ((rep, half * NY + mod(y + 1, NY)), (rep, half * NY + mod(y - 1, NY)))
     zs = [(rep_of(xh, mod(z + d, NZ), core), fs) for d in range(1, NZ)]
-    group = [(rep_of(lax.rem(xh + j // 2, 2), z, lax.rem(core + j % 2, 2)), fs) for j in range(1, 4)]
+    twin = (rep_of(xh, z, 1 - core), fs)
+    other = (rep_of(1 - xh, z, core), fs)
+    near = (partner, *ring, twin, other)
+    white = lax.rem(half + y + core + xh, 2) == 0
+
+    def signal(sem, peer):
+        pl.semaphore_signal(sem, inc=1, device_id=peer, device_id_type=MESH)
 
     barrier = pltpu.get_barrier_semaphore()
-    for peer in (partner, *ring, *zs, *group):
-        pl.semaphore_signal(barrier, inc=1, device_id=peer, device_id_type=MESH)
+
+    @pl.when(jnp.logical_not(white))
+    def _():
+        for peer in near:
+            signal(barrier, peer)
 
     def remote(src, dst, send, recv, peer):
         return pltpu.make_async_remote_copy(src, dst, send, recv, device_id=peer, device_id_type=MESH)
@@ -87,18 +96,26 @@
     ]
     loads = [
         pltpu.make_async_copy(src, dst, local_sem.at[2 + NPAIR + i])
-        for i, (src, dst) in enumerate(((a_ref, an), (om_ref, om), (m1_ref, m1), (m2_ref, m2)))
+        for i, (src, dst) in enumerate(((a_ref, ao.at[0]), (om_ref, ao.at[1]), (m1_ref, m1), (m2_ref, m2)))
     ]
-    for load in (*load_x, *loads):
+    for load in (*loads[:2], *load_x, *loads[2:]):
         load.start()
     load_w.wait()
-    eye = (
-        lax.broadcasted_iota(jnp.int32, (KV, KV), 0) == lax.broadcasted_iota(jnp.int32, (KV, KV), 1)
-    ).astype(BF16)
-    own_w = block(wf, y, (0, ROWS))[...]
-    wt[...] = dot(eye, own_w, ((1,), (1,))).astype(BF16).reshape(2, NZ, 2 * SHARE, ROWS)
     load_c.wait()
-    pl.semaphore_wait(barrier, 3 + len(zs) + len(group))
+    for load in loads[:2]:
+        load.wait()
+
+    @pl.when(white)
+    def _():
+        pl.semaphore_wait(barrier, len(near))
+        for peer in near:
+            signal(hello, peer)
+
+    @pl.when(jnp.logical_not(white))
+    def _():
+        pl.semaphore_wait(hello, len(near))
+        for peer in zs:
+            signal(barrier, peer)
 
     send_c = remote(cm, cp, xs.at[0], xr.at[0], partner)
     send_x = [
@@ -120,6 +137,14 @@
             return range(AG_SUBS)
         return range(AG_SUBS // 2) if d == 0 else range(AG_SUBS // 2, AG_SUBS)
 
+    def ag_forward(s, js=range(AG_SUBS)):
+        for j in js:
+            for d in range(2):
+                if s > 0 and j in ag_subs(d, s - 1):
+                    ag(d, s - 1, j).wait_recv()
+                if s < NY // 2 and j in ag_subs(d, s):
+                    ag(d, s, j).start()
+
     middle = pl.ds(pl.multiple_of(MID // 2 * odd, 16), MID // 2)
     send_mid = remote(
         wf.at[quad, pl.ds(pl.multiple_of(MID + MID // 2 * odd, 16), MID // 2)], wo.at[quad, middle],
@@ -133,32 +158,14 @@
         return remote(place, place, mid_s.at[d, s], mid_r.at[d, s], ring[d])
 
     def mid_forward(s):
+        if s == 0:
+            send_mid.wait_recv()
         for d in range(2):
             if s > 0:
                 mid(d, s - 1).wait_recv()
             if s < NY // 2:
                 mid(d, s).start()
 
-    send_mid.start()
-    send_c.start()
-    for j in range(AG_SUBS):
-        for d in range(2):
-            ag(d, 0, j).start()
-    send_x[0].start()
-    z1 = [
-        remote(wt.at[:, mod(z + d, NZ)], r1.at[d - 1], z1_s.at[d - 1], z1_r.at[d - 1], zs[d - 1]) for d in range(1, NZ)
-    ]
-    for copy in z1:
-        copy.start()
-
-    def ag_forward(s):
-        for j in range(AG_SUBS):
-            for d in range(2):
-                if j in ag_subs(d, s - 1):
-                    ag(d, s - 1, j).wait_recv()
-                if s < NY // 2 and j in ag_subs(d, s):
-                    ag(d, s, j).start()
-
     rsub = ROWS // RS_SUBS
 
     def rs(d, s, j):
@@ -167,128 +174,169 @@
             return remote(sb0.at[d, rows], rb0.at[d, rows], rs_s.at[d, s, j], rs_r.at[d, s, j], ring[d])
         return remote(sb.at[d, s - 1, rows], rb.at[d, s - 1, rows], rs_s.at[d, s, j], rs_r.at[d, s, j], ring[d])
 
-    def rs_step(s):
-        for j in range(RS_SUBS):
+    def rs_step(s, js=range(RS_SUBS)):
+        for j in js:
             rows = pl.ds(j * rsub, rsub)
             for d in range(2):
                 dest = mod(y + 4 - s, NY) if d == 0 else mod(y - 4 + s, NY)
                 own = block(part, dest, (j * rsub, rsub))
-                near = pl.ds(d * (KV // 2), KV // 2)
-                far = pl.ds((1 - d) * (KV // 2), KV // 2)
+                here = pl.ds(d * (KV // 2), KV // 2)
+                there = pl.ds((1 - d) * (KV // 2), KV // 2)
                 if s == 0:
-                    sb0[d, rows] = own[:, near].astype(BF16)
+                    sb0[d, rows] = own[:, here].astype(BF16)
                 elif s == 1:
                     rs(d, 0, j).wait_recv()
-                    sb[d, 0, rows, near] = (own[:, near] + rb0[d, rows].astype(F32)).astype(BF16)
-                    sb[d, 0, rows, far] = own[:, far].astype(BF16)
+                    sb[d, 0, rows, here] = (own[:, here] + rb0[d, rows].astype(F32)).astype(BF16)
+                    sb[d, 0, rows, there] = own[:, there].astype(BF16)
                 else:
                     rs(d, s - 1, j).wait_recv()
                     sb[d, s - 1, rows] = (own[...] + rb[d, s - 2, rows].astype(F32)).astype(BF16)
                 rs(d, s, j).start()
 
     def make_part(i):
+        if i == 0:
+            send_c.wait_recv()
         load_x[i].wait()
         send_x[i].wait_recv()
         part[order[i]] = dot(xo[order[i]], cm[...], ((0,), (0,))) + dot(xp[order[i]], cp[...], ((0,), (0,)))
 
+    z1 = [remote(wt.at[mod(z + d, NZ)], r1.at[d - 1], z1_s.at[d - 1], z1_r.at[d - 1], zs[d - 1]) for d in range(1, NZ)]
+    g2 = remote(s1.at[1 - core], r2, g_s.at[0], g_r.at[0], twin)
+    g3 = remote(s2, r3, g_s.at[1], g_r.at[1], other)
+    mine = fa.at[z, core]
+    z4 = [remote(mine, mine, z4_s.at[d], z4_r.at[d], zs[d]) for d in range(NZ - 1)]
+    g5 = remote(fa.at[:, core], fa.at[:, core], g_s.at[2], g_r.at[2], twin)
+    swap = remote(ao, aop, g_s.at[3], g_r.at[3], other)
+
+    def transpose_weight():
+        size = KV // 2
+        eye = (
+            lax.broadcasted_iota(jnp.int32, (size, size), 0) == lax.broadcasted_iota(jnp.int32, (size, size), 1)
+        ).astype(BF16)
+        own_w = block(wf, y, (0, ROWS))[...]
+        stacked = jnp.concatenate([own_w[:, :size], own_w[:, size:]], axis=0)
+        wt[...] = dot(eye, stacked, ((1,), (1,))).astype(BF16).reshape(NZ, 2 * SHARE, 2 * ROWS)
+
+    def z_ready():
+        @pl.when(jnp.logical_not(white))
+        def _():
+            pl.semaphore_wait(barrier, len(zs))
+            signal(ready, partner)
+
+        @pl.when(white)
+        def _():
+            pl.semaphore_wait(ready, 1)
+
+        for copy in z1:
+            copy.start()
+
+    def sum_z():
+        for copy in z1:
+            copy.wait_recv()
+        total = wt[z].astype(F32)
+        for d in range(NZ - 1):
+            total = total + r1[d].astype(F32)
+        s1[...] = total.reshape(2, SHARE, 2 * ROWS)
+        g2.start()
+
+    def sum_core():
+        g2.wait_recv()
+        s2[...] = s1[core] + r2[...]
+        g3.start()
+
+    def outer():
+        g3.wait_recv()
+        swap.wait_recv()
+
+        def both(k):
+            first = jnp.where(xh == 0, ao[k], aop[k])
+            second = jnp.where(xh == 0, aop[k], ao[k])
+            return jnp.concatenate([first, second], axis=1)
+
+        anchor = both(0)
+        delta = anchor - (s2[...] + r3[...]) / (2 * NZ * 2)
+        new_momentum = outer_mu * both(1) + delta
+        new_anchor = anchor - outer_rate * (delta + outer_mu * new_momentum)
+        nm_ref[...] = jnp.where(xh == 0, new_momentum[:, :ROWS], new_momentum[:, ROWS:])
+        na_ref[...] = jnp.where(xh == 0, new_anchor[:, :ROWS], new_anchor[:, ROWS:])
+        mine[...] = new_anchor
+        for copy in z4:
+            copy.start()
+
+    def share_core():
+        for copy in z4:
+            copy.wait_recv()
+        g5.start()
+
+    def make_ig_partner():
+        for i in range(NPAIR):
+            for k, rows in enumerate((pl.ds(0, SIDE // 2), pl.ds(PAIR - SIDE // 2, SIDE // 2))):
+                igs[i, :, k * (SIDE // 2) : (k + 1) * (SIDE // 2)] = dot(cp[...], wf[i, rows], ((1,), (1,))).astype(BF16)
+            send_ig[i].start()
+
+    def make_ig_own():
+        for i in range(NPAIR):
+            ig_own[i] = dot(cm[...], wf[i], ((1,), (1,))).astype(BF16)
+            ig_mid[i] = dot(cm[...], wo[i], ((1,), (1,))).astype(BF16)
+
+    def finish():
+        for load in loads[2:]:
+            load.wait()
+        g5.wait_recv()
+        turned = fa[...].reshape(KV // 2, 2 * ROWS).T
+        full_anchor = jnp.concatenate([turned[:ROWS], turned[ROWS:]], axis=1)
+        for j in range(RS_SUBS):
+            rows = pl.ds(j * rsub, rsub)
+            for d in range(2):
+                rs(d, 3, j).wait_recv()
+            gradient = block(part, y, (j * rsub, rsub))[...] + rb[0, 2, rows].astype(F32) + rb[1, 2, rows].astype(F32)
+            new_first = beta_one * m1[rows] + (1.0 - beta_one) * gradient
+            new_second = beta_two * m2[rows] + (1.0 - beta_two) * gradient * gradient
+            nf_ref[rows] = new_first
+            ns_ref[rows] = new_second
+            weights = block(wf, y, (j * rsub, rsub))[...].astype(F32)
+            update = new_first / (jnp.sqrt(new_second) + adam_eps)
+            inner = weights - learn_rate * (update + decay_rate * weights)
+            blend = blend_keep * inner + (1.0 - blend_keep) * full_anchor[j * rsub : (j + 1) * rsub]
+            nw_ref[rows] = blend.astype(BF16)
+
+    send_mid.start()
+    send_c.start()
+    ag_forward(0)
+    send_x[0].start()
+    swap.start()
+    transpose_weight()
     ag_forward(1)
-    send_mid.wait_recv()
     mid_forward(0)
-
-    for copy in z1:
-        copy.wait_recv()
-    total = wt[:, pl.ds(z, 1)].astype(F32).reshape(2, 2 * SHARE, ROWS)
-    for d in range(NZ - 1):
-        total = total + r1[d].astype(F32)
-    s1[...] = total.reshape(2, 2, SHARE, ROWS)
-    g2 = [
-        remote(
-            s1.at[lax.rem(xh + j // 2, 2), lax.rem(core + j % 2, 2)], r2.at[j - 1],
-            g2_s.at[j - 1], g2_r.at[j - 1], group[j - 1],
-        )
-        for j in range(1, 4)
-    ]
-    for copy in g2:
-        copy.start()
+    z_ready()
     send_x[1].start()
-
     ag_forward(2)
-    mid_forward(1)
-    send_c.wait_recv()
     make_part(0)
     rs_step(0)
     send_x[2].start()
-
-    for copy in g2:
-        copy.wait_recv()
-    for load in loads[:2]:
-        load.wait()
-    share = s1[pl.ds(xh, 1), pl.ds(core, 1)].reshape(SHARE, ROWS)
-    share = share + r2[0] + r2[1] + r2[2]
-    anchor = an[...]
-    delta = anchor - share / (2 * NZ * 2)
-    new_momentum = outer_mu * om[...] + delta
-    new_anchor = anchor - outer_rate * (delta + outer_mu * new_momentum)
-    nm_ref[...] = new_momentum
-    na_ref[...] = new_anchor
-    fa[pl.ds(xh, 1), pl.ds(z, 1), pl.ds(core, 1)] = new_anchor[None, None, None]
-    mine = fa.at[xh, z, core]
-    g3 = [remote(mine, mine, g3_s.at[j], g3_r.at[j], group[j]) for j in range(3)]
-    for copy in g3:
-        copy.start()
+    mid_forward(1)
+    ag_forward(3)
+    sum_z()
+    make_part(1)
+    sum_core()
     send_x[3].start()
-
-    ag_forward(3)
+    rs_step(1)
     mid_forward(2)
-    make_part(1)
-    rs_step(1)
-    for copy in g3:
-        copy.wait_recv()
-    layer = fa.at[:, z]
-    z4 = [remote(layer, layer, z4_s.at[d], z4_r.at[d], zs[d]) for d in range(NZ - 1)]
-    for copy in z4:
-        copy.start()
-
+    outer()
     ag_forward(4)
-    mid_forward(3)
-    for i in range(NPAIR):
-        for k, rows in enumerate((pl.ds(0, SIDE // 2), pl.ds(PAIR - SIDE // 2, SIDE // 2))):
-            igs[i, :, k * (SIDE // 2) : (k + 1) * (SIDE // 2)] = dot(cp[...], wf[i, rows], ((1,), (1,))).astype(BF16)
-        send_ig[i].start()
-
+    make_ig_partner()
     make_part(2)
     rs_step(2)
+    mid_forward(3)
     make_part(3)
     rs_step(3)
-    for i in range(NPAIR):
-        ig_own[i] = dot(cm[...], wf[i], ((1,), (1,))).astype(BF16)
+    share_core()
     mid_forward(4)
-    for i in range(NPAIR):
-        ig_mid[i] = dot(cm[...], wo[i], ((1,), (1,))).astype(BF16)
-
-    for load in loads[2:]:
-        load.wait()
-    for copy in z4:
-        copy.wait_recv()
-    full_anchor = fa[...].reshape(KV, ROWS).T
-    for j in range(RS_SUBS):
-        rows = pl.ds(j * rsub, rsub)
-        for d in range(2):
-            rs(d, 3, j).wait_recv()
-        gradient = block(part, y, (j * rsub, rsub))[...] + rb[0, 2, rows].astype(F32) + rb[1, 2, rows].astype(F32)
-        new_first = beta_one * m1[rows] + (1.0 - beta_one) * gradient
-        new_second = beta_two * m2[rows] + (1.0 - beta_two) * gradient * gradient
-        nf_ref[rows] = new_first
-        ns_ref[rows] = new_second
-        weights = block(wf, y, (j * rsub, rsub))[...].astype(F32)
-        update = new_first / (jnp.sqrt(new_second) + adam_eps)
-        inner = weights - learn_rate * (update + decay_rate * weights)
-        blend = blend_keep * inner + (1.0 - blend_keep) * full_anchor[j * rsub : (j + 1) * rsub]
-        nw_ref[rows] = blend.astype(BF16)
-
+    make_ig_own()
+    finish()
     for copy in send_ig:
         copy.wait_recv()
-    for copy in (send_mid, send_c, *send_x, *send_ig, *z1, *g2, *g3, *z4):
+    for copy in (send_mid, send_c, *send_x, *send_ig, *z1, g2, g3, *z4, g5, swap):
         copy.wait_send()
     for s in range(NY // 2):
         for d in range(2):
@@ -347,13 +395,15 @@
             pltpu.VMEM((2, ROWS, KV // 2), BF16),
             pltpu.VMEM((2, 3, ROWS, KV), BF16),
             pltpu.VMEM((NPAIR, TOK, SIDE), BF16),
-            pltpu.VMEM((2, NZ, 2 * SHARE, ROWS), BF16),
-            pltpu.VMEM((NZ - 1, 2, 2 * SHARE, ROWS), BF16),
-            pltpu.VMEM((2, 2, SHARE, ROWS), F32),
-            pltpu.VMEM((3, SHARE, ROWS), F32),
-            pltpu.VMEM((2, NZ, 2, SHARE, ROWS), F32),
-            pltpu.VMEM((SHARE, ROWS), F32),
-            pltpu.VMEM((SHARE, ROWS), F32),
+            pltpu.VMEM((NZ, 2 * SHARE, 2 * ROWS), BF16),
+            pltpu.VMEM((NZ - 1, 2 * SHARE, 2 * ROWS), BF16),
+            pltpu.VMEM((2, SHARE, 2 * ROWS), F32),
+            pltpu.VMEM((SHARE, 2 * ROWS), F32),
+            pltpu.VMEM((SHARE, 2 * ROWS), F32),
+            pltpu.VMEM((SHARE, 2 * ROWS), F32),
+            pltpu.VMEM((2, SHARE, ROWS), F32),
+            pltpu.VMEM((2, SHARE, ROWS), F32),
+            pltpu.VMEM((NZ, 2, SHARE, 2 * ROWS), F32),
             pltpu.VMEM((ROWS, KV), F32),
             pltpu.VMEM((ROWS, KV), F32),
             dma((2 + NPAIR + 4,)),
@@ -362,9 +412,9 @@
             dma((2, NY // 2)), dma((2, NY // 2)),
             dma((2, NY // 2, RS_SUBS)), dma((2, NY // 2, RS_SUBS)),
             dma((NZ - 1,)), dma((NZ - 1,)),
-            dma((3,)), dma((3,)),
-            dma((3,)), dma((3,)),
             dma((NZ - 1,)), dma((NZ - 1,)),
+            dma((4,)), dma((4,)),
+            pltpu.SemaphoreType.REGULAR, pltpu.SemaphoreType.REGULAR,
         ],
         compiler_params=pltpu.CompilerParams(
             collective_id=0, has_side_effects=True, vmem_limit_bytes=40 << 20

time: 53.6 us -> 50.2 us (0.937)
  Pallas kernels: 52.8 us -> 49.5 us
    pallas_call x1, Pallas kernels: 51.2 us -> 47.8 us  [body(): pl.pallas_call(step_kernel, out_shape=(shape((NPAIR, TOK, PAIR), BF16), s...]
where the time goes in v3:
time: 50.2 us; the launch traced here: 50.1 us
  Pallas kernels  49.5 us (99%)
  between operations  0.66 us (1%)
    pallas_call x1, Pallas kernels, body(): pl.pallas_call(step_kernel, out_shape=(shape((NPAIR, TOK, PAIR), BF16), s...  47.8 us
    pallas_call x1, Pallas kernels, body(): pl.pallas_call(write_kernel, out_shape=(shape((TOK, D), BF16), shape((ROW...  1.62 us

profile of v3, /device:TPU:1, one launch (start us, length us, event | category | flops | bytes accessed | tf_op | source)
XLA Modules:
  0.0 50.1 jit_solution(4543745633946752201)
XLA Ops:
  0.6 47.8 %step.1 = (bf16[4,240,384]{2,1,0:T(8,128)(2,1)S(1)}, bf16[4,240,256]{2,1,0:T(8,128)(2,1)S(1)}, bf16[4,240,128]{2,1,0:T(8,128)(2,1)S(1)}, bf16[192,512]{1,0:T(8,1...) custom-call(bf16[240,3072]{1,0:T(8,128)(2,1)} %x_ref.1, ...), custom_call_target="tpu_custom_call" | custom-call | flops 1600000000 | bytes 5000000 | tf_op jit(solution)/shard_map/step/pallas_call | solution.py:377
  48.5 1.6 %write.1 = (bf16[240,3072]{1,0:T(8,128)(2,1)}, bf16[192,512]{1,0:T(8,128)(2,1)}, f32[192,512]{1,0:T(8,128)}, f32[192,512]{1,0:T(8,128)}, f32[16,192]{1,0:T(8,128)}, /*index=5*/f32[16,192]{1,0:T(8,128)}) custom-call(s32[1]{0:T(128)} %bitcast.half_ref, bf16[4,240,384]{2,1,0:T(8,128)(2,1)S(1)} %get-tuple-element.20.ig_own, ...), custom_call_target="tpu_custom_call" | custom-call | tf_op jit(solution)/shard_map/write/pallas_call | solution.py:433

commit v4 on v3

--- a/solution.py
+++ b/solution.py
@@ -27,6 +27,8 @@
 RS_SUBS = 2
 MID = 128
 SIDE = PAIR - MID
+X_PIECES = [(0, pl.ds(0, TOK)), (1, pl.ds(0, TOK)), (2, pl.ds(0, TOK)), (3, pl.ds(0, 128)), (3, pl.ds(128, TOK - 128))]
+LATE = 4
 SHARE = 16
 F32 = jnp.float32
 BF16 = jnp.bfloat16
@@ -43,7 +45,7 @@
 def step_kernel(
     x_ref, c_ref, w_ref, m1_ref, m2_ref, a_ref, om_ref,
     ig_own, ig_recv, ig_mid, nw_ref, nf_ref, ns_ref, na_ref, nm_ref,
-    xo, xp, cm, cp, wf, wo, part, sb0, sb, rb0, rb, igs, wt, r1, s1, r2, s2, r3, ao, aop, fa, m1, m2,
+    xo, xp, cm, cp, wf, wo, part, sb0, sb, rb0, rb, igs, wt, r1, s1, r2, ao, aop, fa, m1, m2,
     local_sem, xs, xr, ag_s, ag_r, mid_s, mid_r, rs_s, rs_r, z1_s, z1_r, z4_s, z4_r, g_s, g_r, hello, ready,
 ):
     rep = lax.axis_index("replica")
@@ -59,11 +61,15 @@
     zs = [(rep_of(xh, mod(z + d, NZ), core), fs) for d in range(1, NZ)]
     twin = (rep_of(xh, z, 1 - core), fs)
     other = (rep_of(1 - xh, z, core), fs)
-    near = (partner, *ring, twin, other)
-    white = lax.rem(half + y + core + xh, 2) == 0
+    cross = (rep_of(1 - xh, z, 1 - core), fs)
+    near = (partner, *ring)
+    far = (*zs, twin, other, cross)
+    white = lax.rem(half + y, 2) == 0
 
     def signal(sem, peer):
         pl.semaphore_signal(sem, inc=1, device_id=peer, device_id_type=MESH)
+
+    early, late = z < LATE, z >= LATE
 
     barrier = pltpu.get_barrier_semaphore()
 
@@ -102,8 +108,6 @@
         load.start()
     load_w.wait()
     load_c.wait()
-    for load in loads[:2]:
-        load.wait()
 
     @pl.when(white)
     def _():
@@ -114,16 +118,18 @@
     @pl.when(jnp.logical_not(white))
     def _():
         pl.semaphore_wait(hello, len(near))
-        for peer in zs:
+        for peer in far:
             signal(barrier, peer)
 
     send_c = remote(cm, cp, xs.at[0], xr.at[0], partner)
     send_x = [
-        remote(x_ref.at[:, pair_columns(1 - half, order[i])], xp.at[order[i]], xs.at[1 + i], xr.at[1 + i], partner)
-        for i in range(NPAIR)
+        remote(
+            x_ref.at[rows, pair_columns(1 - half, order[i])], xp.at[order[i], rows], xs.at[1 + k], xr.at[1 + k], partner
+        )
+        for k, (i, rows) in enumerate(X_PIECES)
     ]
     send_ig = [
-        remote(igs.at[i], ig_recv.at[i], xs.at[1 + NPAIR + i], xr.at[1 + NPAIR + i], partner) for i in range(NPAIR)
+        remote(igs.at[i], ig_recv.at[i], xs.at[2 + NPAIR + i], xr.at[2 + NPAIR + i], partner) for i in range(NPAIR)
     ]
 
     sub = ROWS // AG_SUBS
@@ -148,7 +154,7 @@
     middle = pl.ds(pl.multiple_of(MID // 2 * odd, 16), MID // 2)
     send_mid = remote(
         wf.at[quad, pl.ds(pl.multiple_of(MID + MID // 2 * odd, 16), MID // 2)], wo.at[quad, middle],
-        xs.at[1 + 2 * NPAIR], xr.at[1 + 2 * NPAIR], partner,
+        xs.at[2 + 2 * NPAIR], xr.at[2 + 2 * NPAIR], partner,
     )
 
     def mid(d, s):
@@ -197,16 +203,20 @@
         if i == 0:
             send_c.wait_recv()
         load_x[i].wait()
-        send_x[i].wait_recv()
+        for copy, (pair, _) in zip(send_x, X_PIECES):
+            if pair == i:
+                copy.wait_recv()
         part[order[i]] = dot(xo[order[i]], cm[...], ((0,), (0,))) + dot(xp[order[i]], cp[...], ((0,), (0,)))
 
     z1 = [remote(wt.at[mod(z + d, NZ)], r1.at[d - 1], z1_s.at[d - 1], z1_r.at[d - 1], zs[d - 1]) for d in range(1, NZ)]
-    g2 = remote(s1.at[1 - core], r2, g_s.at[0], g_r.at[0], twin)
-    g3 = remote(s2, r3, g_s.at[1], g_r.at[1], other)
+    g2 = [
+        remote(s1.at[place], r2.at[k], g_s.at[k], g_r.at[k], peer)
+        for k, (place, peer) in enumerate(((1 - core, twin), (core, other), (1 - core, cross)))
+    ]
     mine = fa.at[z, core]
     z4 = [remote(mine, mine, z4_s.at[d], z4_r.at[d], zs[d]) for d in range(NZ - 1)]
-    g5 = remote(fa.at[:, core], fa.at[:, core], g_s.at[2], g_r.at[2], twin)
-    swap = remote(ao, aop, g_s.at[3], g_r.at[3], other)
+    g5 = remote(fa.at[:, core], fa.at[:, core], g_s.at[3], g_r.at[3], twin)
+    swap = remote(ao, aop, g_s.at[4], g_r.at[4], other)
 
     def transpose_weight():
         size = KV // 2
@@ -217,10 +227,10 @@
         stacked = jnp.concatenate([own_w[:, :size], own_w[:, size:]], axis=0)
         wt[...] = dot(eye, stacked, ((1,), (1,))).astype(BF16).reshape(NZ, 2 * SHARE, 2 * ROWS)
 
-    def z_ready():
+    def start_replica():
         @pl.when(jnp.logical_not(white))
         def _():
-            pl.semaphore_wait(barrier, len(zs))
+            pl.semaphore_wait(barrier, len(far))
             signal(ready, partner)
 
         @pl.when(white)
@@ -229,6 +239,9 @@
 
         for copy in z1:
             copy.start()
+        for load in loads[:2]:
+            load.wait()
+        swap.start()
 
     def sum_z():
         for copy in z1:
@@ -237,16 +250,13 @@
         for d in range(NZ - 1):
             total = total + r1[d].astype(F32)
         s1[...] = total.reshape(2, SHARE, 2 * ROWS)
-        g2.start()
-
-    def sum_core():
-        g2.wait_recv()
-        s2[...] = s1[core] + r2[...]
-        g3.start()
+        for copy in g2:
+            copy.start()
 
     def outer():
-        g3.wait_recv()
-        swap.wait_recv()
+        for copy in (*g2, swap):
+            copy.wait_recv()
+        share = s1[core] + r2[0] + r2[1] + r2[2]
 
         def both(k):
             first = jnp.where(xh == 0, ao[k], aop[k])
@@ -254,7 +264,7 @@
             return jnp.concatenate([first, second], axis=1)
 
         anchor = both(0)
-        delta = anchor - (s2[...] + r3[...]) / (2 * NZ * 2)
+        delta = anchor - share / (2 * NZ * 2)
         new_momentum = outer_mu * both(1) + delta
         new_anchor = anchor - outer_rate * (delta + outer_mu * new_momentum)
         nm_ref[...] = jnp.where(xh == 0, new_momentum[:, :ROWS], new_momentum[:, ROWS:])
@@ -304,29 +314,31 @@
     send_c.start()
     ag_forward(0)
     send_x[0].start()
-    swap.start()
     transpose_weight()
+    pl.when(late)(start_replica)
+    mid_forward(0)
     ag_forward(1)
-    mid_forward(0)
-    z_ready()
     send_x[1].start()
+    mid_forward(1)
+    pl.when(early)(start_replica)
     ag_forward(2)
     make_part(0)
     rs_step(0)
+    pl.when(late)(sum_z)
     send_x[2].start()
-    mid_forward(1)
     ag_forward(3)
-    sum_z()
     make_part(1)
-    sum_core()
     send_x[3].start()
     rs_step(1)
+    pl.when(early)(sum_z)
+    send_x[4].start()
+    pl.when(late)(outer)
     mid_forward(2)
-    outer()
     ag_forward(4)
     make_ig_partner()
     make_part(2)
     rs_step(2)
+    pl.when(early)(outer)
     mid_forward(3)
     make_part(3)
     rs_step(3)
@@ -336,7 +348,7 @@
     finish()
     for copy in send_ig:
         copy.wait_recv()
-    for copy in (send_mid, send_c, *send_x, *send_ig, *z1, g2, g3, *z4, g5, swap):
+    for copy in (send_mid, send_c, *send_x, *send_ig, *z1, *g2, *z4, g5, swap):
         copy.wait_send()
     for s in range(NY // 2):
         for d in range(2):
@@ -398,22 +410,20 @@
             pltpu.VMEM((NZ, 2 * SHARE, 2 * ROWS), BF16),
             pltpu.VMEM((NZ - 1, 2 * SHARE, 2 * ROWS), BF16),
             pltpu.VMEM((2, SHARE, 2 * ROWS), F32),
-            pltpu.VMEM((SHARE, 2 * ROWS), F32),
-            pltpu.VMEM((SHARE, 2 * ROWS), F32),
-            pltpu.VMEM((SHARE, 2 * ROWS), F32),
+            pltpu.VMEM((3, SHARE, 2 * ROWS), F32),
             pltpu.VMEM((2, SHARE, ROWS), F32),
             pltpu.VMEM((2, SHARE, ROWS), F32),
             pltpu.VMEM((NZ, 2, SHARE, 2 * ROWS), F32),
             pltpu.VMEM((ROWS, KV), F32),
             pltpu.VMEM((ROWS, KV), F32),
             dma((2 + NPAIR + 4,)),
-            dma((2 + 2 * NPAIR,)), dma((2 + 2 * NPAIR,)),
+            dma((3 + 2 * NPAIR,)), dma((3 + 2 * NPAIR,)),
             dma((2, NY // 2, AG_SUBS)), dma((2, NY // 2, AG_SUBS)),
             dma((2, NY // 2)), dma((2, NY // 2)),
             dma((2, NY // 2, RS_SUBS)), dma((2, NY // 2, RS_SUBS)),
             dma((NZ - 1,)), dma((NZ - 1,)),
             dma((NZ - 1,)), dma((NZ - 1,)),
-            dma((4,)), dma((4,)),
+            dma((5,)), dma((5,)),
             pltpu.SemaphoreType.REGULAR, pltpu.SemaphoreType.REGULAR,
         ],
         compiler_params=pltpu.CompilerParams(

time: 50.2 us -> 48.1 us (0.958)
  Pallas kernels: 49.5 us -> 47.3 us
    pallas_call x1, Pallas kernels: 47.8 us -> 45.7 us  [body(): pl.pallas_call(step_kernel, out_shape=(shape((NPAIR, TOK, PAIR), BF16), s...]
where the time goes in v4:
time: 48.1 us; the launch traced here: 48 us
  Pallas kernels  47.3 us (98%)
  between operations  0.66 us (1%)
    pallas_call x1, Pallas kernels, body(): pl.pallas_call(step_kernel, out_shape=(shape((NPAIR, TOK, PAIR), BF16), s...  45.7 us
    pallas_call x1, Pallas kernels, body(): pl.pallas_call(write_kernel, out_shape=(shape((TOK, D), BF16), shape((ROW...  1.62 us

profile of v4, /device:TPU:1, one launch (start us, length us, event | category | flops | bytes accessed | tf_op | source)
XLA Modules:
  0.0 48.0 jit_solution(17037451809512093923)
XLA Ops:
  0.6 45.7 %step.1 = (bf16[4,240,384]{2,1,0:T(8,128)(2,1)S(1)}, bf16[4,240,256]{2,1,0:T(8,128)(2,1)S(1)}, bf16[4,240,128]{2,1,0:T(8,128)(2,1)S(1)}, bf16[192,512]{1,0:T(8,1...) custom-call(bf16[240,3072]{1,0:T(8,128)(2,1)} %x_ref.1, ...), custom_call_target="tpu_custom_call" | custom-call | flops 1600000000 | bytes 5000000 | tf_op jit(solution)/shard_map/step/pallas_call | solution.py:389
  46.4 1.6 %write.1 = (bf16[240,3072]{1,0:T(8,128)(2,1)}, bf16[192,512]{1,0:T(8,128)(2,1)}, f32[192,512]{1,0:T(8,128)}, f32[192,512]{1,0:T(8,128)}, f32[16,192]{1,0:T(8,128)}, /*index=5*/f32[16,192]{1,0:T(8,128)}) custom-call(s32[1]{0:T(128)} %bitcast.half_ref, bf16[4,240,384]{2,1,0:T(8,128)(2,1)S(1)} %get-tuple-element.20.ig_own, ...), custom_call_target="tpu_custom_call" | custom-call | tf_op jit(solution)/shard_map/write/pallas_call | solution.py:443

commit v5 on v4

--- a/solution.py
+++ b/solution.py
@@ -69,7 +69,9 @@
     def signal(sem, peer):
         pl.semaphore_signal(sem, inc=1, device_id=peer, device_id_type=MESH)
 
-    early, late = z < LATE, z >= LATE
+    late, first = z >= LATE, rep + fs == 0
+    early = jnp.logical_not(jnp.logical_or(late, first))
+    not_early = jnp.logical_or(late, first)
 
     barrier = pltpu.get_barrier_semaphore()
 
@@ -314,17 +316,18 @@
     send_c.start()
     ag_forward(0)
     send_x[0].start()
+    send_x[1].start()
     transpose_weight()
     pl.when(late)(start_replica)
     mid_forward(0)
     ag_forward(1)
-    send_x[1].start()
+    pl.when(first)(start_replica)
     mid_forward(1)
     pl.when(early)(start_replica)
     ag_forward(2)
     make_part(0)
     rs_step(0)
-    pl.when(late)(sum_z)
+    pl.when(not_early)(sum_z)
     send_x[2].start()
     ag_forward(3)
     make_part(1)
@@ -332,7 +335,7 @@
     rs_step(1)
     pl.when(early)(sum_z)
     send_x[4].start()
-    pl.when(late)(outer)
+    pl.when(not_early)(outer)
     mid_forward(2)
     ag_forward(4)
     make_ig_partner()
@@ -345,18 +348,23 @@
     share_core()
     mid_forward(4)
     make_ig_own()
-    finish()
-    for copy in send_ig:
-        copy.wait_recv()
-    for copy in (send_mid, send_c, *send_x, *send_ig, *z1, *g2, *z4, g5, swap):
+    for copy in (send_mid, send_c, *send_x, *z1, *g2, swap):
         copy.wait_send()
     for s in range(NY // 2):
         for d in range(2):
             mid(d, s).wait_send()
             for j in ag_subs(d, s):
                 ag(d, s, j).wait_send()
-            for j in range(RS_SUBS):
+            for j in range(RS_SUBS if s < NY // 2 - 1 else 0):
                 rs(d, s, j).wait_send()
+    finish()
+    for copy in send_ig:
+        copy.wait_recv()
+    for copy in (*send_ig, *z4, g5):
+        copy.wait_send()
+    for d in range(2):
+        for j in range(RS_SUBS):
+            rs(d, NY // 2 - 1, j).wait_send()
 
 
 def write_kernel(half_ref, ig_own, ig_recv, ig_mid, nw, nf, ns, na, nm, o_ig, o_nw, o_nf, o_ns, o_na, o_nm, sem):

time: 48.1 us -> 48 us (level)
  no operation moved by 1% of the time
where the time goes in v5:
time: 48 us; the launch traced here: 47.9 us
  Pallas kernels  47.2 us (98%)
  between operations  0.66 us (1%)
    pallas_call x1, Pallas kernels, body(): pl.pallas_call(step_kernel, out_shape=(shape((NPAIR, TOK, PAIR), BF16), s...  45.6 us
    pallas_call x1, Pallas kernels, body(): pl.pallas_call(write_kernel, out_shape=(shape((TOK, D), BF16), shape((ROW...  1.62 us

profile of v5, /device:TPU:1, one launch (start us, length us, event | category | flops | bytes accessed | tf_op | source)
XLA Modules:
  0.0 47.9 jit_solution(11210392103679068392)
XLA Ops:
  0.6 45.6 %step.1 = (bf16[4,240,384]{2,1,0:T(8,128)(2,1)S(1)}, bf16[4,240,256]{2,1,0:T(8,128)(2,1)S(1)}, bf16[4,240,128]{2,1,0:T(8,128)(2,1)S(1)}, bf16[192,512]{1,0:T(8,1...) custom-call(bf16[240,3072]{1,0:T(8,128)(2,1)} %x_ref.1, ...), custom_call_target="tpu_custom_call" | custom-call | flops 1600000000 | bytes 5000000 | tf_op jit(solution)/shard_map/step/pallas_call | solution.py:397
  46.3 1.6 %write.1 = (bf16[240,3072]{1,0:T(8,128)(2,1)}, bf16[192,512]{1,0:T(8,128)(2,1)}, f32[192,512]{1,0:T(8,128)}, f32[192,512]{1,0:T(8,128)}, f32[16,192]{1,0:T(8,128)}, /*index=5*/f32[16,192]{1,0:T(8,128)}) custom-call(s32[1]{0:T(128)} %bitcast.half_ref, bf16[4,240,384]{2,1,0:T(8,128)(2,1)S(1)} %get-tuple-element.20.ig_own, ...), custom_call_target="tpu_custom_call" | custom-call | tf_op jit(solution)/shard_map/write/pallas_call | solution.py:451

commit v6 on v5

--- a/solution.py
+++ b/solution.py
@@ -45,7 +45,7 @@
 def step_kernel(
     x_ref, c_ref, w_ref, m1_ref, m2_ref, a_ref, om_ref,
     ig_own, ig_recv, ig_mid, nw_ref, nf_ref, ns_ref, na_ref, nm_ref,
-    xo, xp, cm, cp, wf, wo, part, sb0, sb, rb0, rb, igs, wt, r1, s1, r2, ao, aop, fa, m1, m2,
+    xo, xp, cm, cp, wf, wo, part, sb0, sb, rb0, rb, igs, igm, wt, r1, s1, r2, ao, fixed, fa, m1, m2,
     local_sem, xs, xr, ag_s, ag_r, mid_s, mid_r, rs_s, rs_r, z1_s, z1_r, z4_s, z4_r, g_s, g_r, hello, ready,
 ):
     rep = lax.axis_index("replica")
@@ -133,6 +133,7 @@
     send_ig = [
         remote(igs.at[i], ig_recv.at[i], xs.at[2 + NPAIR + i], xr.at[2 + NPAIR + i], partner) for i in range(NPAIR)
     ]
+    send_ig.append(remote(igm, ig_mid.at[order[0]], xs.at[3 + 2 * NPAIR], xr.at[3 + 2 * NPAIR], partner))
 
     sub = ROWS // AG_SUBS
 
@@ -161,18 +162,21 @@
 
     def mid(d, s):
         b = mod(y - s, NY) if d == 0 else mod(y + s, NY)
-        start, size = (0, MID // 2) if s < NY // 2 - 1 else (d * (MID // 4), MID // 4)
-        place = wo.at[b // 2, pl.ds(pl.multiple_of(lax.rem(b, 2) * (MID // 2) + start, 16), size)]
+        place = wo.at[b // 2, pl.ds(pl.multiple_of(lax.rem(b, 2) * (MID // 2), 16), MID // 2)]
         return remote(place, place, mid_s.at[d, s], mid_r.at[d, s], ring[d])
 
     def mid_forward(s):
         if s == 0:
             send_mid.wait_recv()
         for d in range(2):
-            if s > 0:
+            if s in (1, 2):
                 mid(d, s - 1).wait_recv()
-            if s < NY // 2:
+            elif s == 3:
+                pl.when(odd == 1 - d)(mid(d, 2).wait_recv)
+            if s < 2:
                 mid(d, s).start()
+            elif s == 2:
+                pl.when(odd == d)(mid(d, 2).start)
 
     rsub = ROWS // RS_SUBS
 
@@ -218,7 +222,7 @@
     mine = fa.at[z, core]
     z4 = [remote(mine, mine, z4_s.at[d], z4_r.at[d], zs[d]) for d in range(NZ - 1)]
     g5 = remote(fa.at[:, core], fa.at[:, core], g_s.at[3], g_r.at[3], twin)
-    swap = remote(ao, aop, g_s.at[4], g_r.at[4], other)
+    swap = remote(fixed.at[0], fixed.at[1], g_s.at[4], g_r.at[4], other)
 
     def transpose_weight():
         size = KV // 2
@@ -243,6 +247,7 @@
             copy.start()
         for load in loads[:2]:
             load.wait()
+        fixed[0] = ao[0] - outer_rate * ((1.0 + outer_mu) * ao[0] + outer_mu * outer_mu * ao[1])
         swap.start()
 
     def sum_z():
@@ -260,17 +265,18 @@
             copy.wait_recv()
         share = s1[core] + r2[0] + r2[1] + r2[2]
 
-        def both(k):
-            first = jnp.where(xh == 0, ao[k], aop[k])
-            second = jnp.where(xh == 0, aop[k], ao[k])
-            return jnp.concatenate([first, second], axis=1)
-
-        anchor = both(0)
-        delta = anchor - share / (2 * NZ * 2)
-        new_momentum = outer_mu * both(1) + delta
-        new_anchor = anchor - outer_rate * (delta + outer_mu * new_momentum)
-        nm_ref[...] = jnp.where(xh == 0, new_momentum[:, :ROWS], new_momentum[:, ROWS:])
-        na_ref[...] = jnp.where(xh == 0, new_anchor[:, :ROWS], new_anchor[:, ROWS:])
+        mean = share / (2 * NZ * 2)
+        mean_own = jnp.where(xh == 0, mean[:, :ROWS], mean[:, ROWS:])
+        delta = ao[0] - mean_own
+        new_momentum = outer_mu * ao[1] + delta
+        own_anchor = ao[0] - outer_rate * (delta + outer_mu * new_momentum)
+        nm_ref[...] = new_momentum
+        na_ref[...] = own_anchor
+        mean_other = jnp.where(xh == 0, mean[:, ROWS:], mean[:, :ROWS])
+        other_anchor = fixed[1] + (outer_rate * (1.0 + outer_mu)) * mean_other
+        first = jnp.where(xh == 0, own_anchor, other_anchor)
+        second = jnp.where(xh == 0, other_anchor, own_anchor)
+        new_anchor = jnp.concatenate([first, second], axis=1)
         mine[...] = new_anchor
         for copy in z4:
             copy.start()
@@ -285,11 +291,14 @@
             for k, rows in enumerate((pl.ds(0, SIDE // 2), pl.ds(PAIR - SIDE // 2, SIDE // 2))):
                 igs[i, :, k * (SIDE // 2) : (k + 1) * (SIDE // 2)] = dot(cp[...], wf[i, rows], ((1,), (1,))).astype(BF16)
             send_ig[i].start()
+        igm[...] = dot(cp[...], wf[order[0], pl.ds(SIDE // 2, MID)], ((1,), (1,))).astype(BF16)
+        send_ig[NPAIR].start()
 
     def make_ig_own():
         for i in range(NPAIR):
             ig_own[i] = dot(cm[...], wf[i], ((1,), (1,))).astype(BF16)
-            ig_mid[i] = dot(cm[...], wo[i], ((1,), (1,))).astype(BF16)
+        for i in range(1, NPAIR):
+            ig_mid[order[i]] = dot(cm[...], wo[order[i]], ((1,), (1,))).astype(BF16)
 
     def finish():
         for load in loads[2:]:
@@ -352,7 +361,10 @@
         copy.wait_send()
     for s in range(NY // 2):
         for d in range(2):
-            mid(d, s).wait_send()
+            if s < 2:
+                mid(d, s).wait_send()
+            elif s == 2:
+                pl.when(odd == d)(mid(d, 2).wait_send)
             for j in ag_subs(d, s):
                 ag(d, s, j).wait_send()
             for j in range(RS_SUBS if s < NY // 2 - 1 else 0):
@@ -415,6 +427,7 @@
             pltpu.VMEM((2, ROWS, KV // 2), BF16),
             pltpu.VMEM((2, 3, ROWS, KV), BF16),
             pltpu.VMEM((NPAIR, TOK, SIDE), BF16),
+            pltpu.VMEM((TOK, MID), BF16),
             pltpu.VMEM((NZ, 2 * SHARE, 2 * ROWS), BF16),
             pltpu.VMEM((NZ - 1, 2 * SHARE, 2 * ROWS), BF16),
             pltpu.VMEM((2, SHARE, 2 * ROWS), F32),
@@ -425,9 +438,9 @@
             pltpu.VMEM((ROWS, KV), F32),
             pltpu.VMEM((ROWS, KV), F32),
             dma((2 + NPAIR + 4,)),
-            dma((3 + 2 * NPAIR,)), dma((3 + 2 * NPAIR,)),
+            dma((4 + 2 * NPAIR,)), dma((4 + 2 * NPAIR,)),
             dma((2, NY // 2, AG_SUBS)), dma((2, NY // 2, AG_SUBS)),
-            dma((2, NY // 2)), dma((2, NY // 2)),
+            dma((2, 3)), dma((2, 3)),
             dma((2, NY // 2, RS_SUBS)), dma((2, NY // 2, RS_SUBS)),
             dma((NZ - 1,)), dma((NZ - 1,)),
             dma((NZ - 1,)), dma((NZ - 1,)),

time: 48 us -> 48.1 us (level)
  no operation moved by 1% of the time
where the time goes in v6:
time: 48.1 us; the launch traced here: 47.9 us
  Pallas kernels  47.3 us (98%)
  between operations  0.66 us (1%)
    pallas_call x1, Pallas kernels, body(): pl.pallas_call(step_kernel, out_shape=(shape((NPAIR, TOK, PAIR), BF16), s...  45.7 us
    pallas_call x1, Pallas kernels, body(): pl.pallas_call(write_kernel, out_shape=(shape((TOK, D), BF16), shape((ROW...  1.62 us

profile of v6, /device:TPU:1, one launch (start us, length us, event | category | flops | bytes accessed | tf_op | source)
XLA Modules:
  0.0 47.9 jit_solution(15572523145046365203)
XLA Ops:
  0.6 45.7 %step.1 = (bf16[4,240,384]{2,1,0:T(8,128)(2,1)S(1)}, bf16[4,240,256]{2,1,0:T(8,128)(2,1)S(1)}, bf16[4,240,128]{2,1,0:T(8,128)(2,1)S(1)}, bf16[192,512]{1,0:T(8,1...) custom-call(bf16[240,3072]{1,0:T(8,128)(2,1)} %x_ref.1, ...), custom_call_target="tpu_custom_call" | custom-call | flops 1600000000 | bytes 5000000 | tf_op jit(solution)/shard_map/step/pallas_call | solution.py:409
  46.3 1.6 %write.1 = (bf16[240,3072]{1,0:T(8,128)(2,1)}, bf16[192,512]{1,0:T(8,128)(2,1)}, f32[192,512]{1,0:T(8,128)}, f32[192,512]{1,0:T(8,128)}, f32[16,192]{1,0:T(8,128)}, /*index=5*/f32[16,192]{1,0:T(8,128)}) custom-call(s32[1]{0:T(128)} %bitcast.half_ref, bf16[4,240,384]{2,1,0:T(8,128)(2,1)S(1)} %get-tuple-element.20.ig_own, ...), custom_call_target="tpu_custom_call" | custom-call | tf_op jit(solution)/shard_map/write/pallas_call | solution.py:464
